TPU v7x, 256 devices: a whole 4x4x8 slice. The times are simulated.
256 devices in a mesh: ctx: 8 (over z), head: 32 (over x, y, core).
Axes of the slice: x: 4, y: 4, z: 8, core: 2. Of those that a mesh axis runs over, the one named last changes fastest.
Arguments:
- queries: bfloat16 [16384, 4096], P('ctx', 'head'), may hold values from -6 to 6
- keys: bfloat16 [16384, 1024], P('ctx', 'head'), may hold values from -6 to 6
- values: bfloat16 [16384, 1024], P('ctx', 'head'), may hold values from -6 to 6
- out_weight: bfloat16 [4096, 4096], P('head'), may hold values from -1.5 to 1.5
- doc_starts: int32 [16], replicated, may hold values from 0 to 16383, as said below
Outputs:
- mixed: bfloat16 [16384, 4096], P(('ctx', 'head'))
Inputs may be any that keep to these rules, and one draw needn't show every extreme that they name: doc_starts[0] is 0, the entries rise strictly, the last is 16383.
All inputs are finite; a program needn't handle non-finite values.
Results may differ from a plain program's by a relative error of at most 0.024.
Values may be sent and summed in bfloat16 or wider, within the bound.
A program may use at most 128 MiB of HBM per device.

v0:
```python
import jax
import jax.numpy as jnp
from jax import lax
from jax.sharding import PartitionSpec as P

GROUP = 4
WINDOW = 4096


def from_partner(value, axis, stride):
    mask = 2**stride
    pairs = [(source, source ^ mask) for source in range(lax.axis_size(axis))]
    return lax.ppermute(value, axis, pairs)


def shifted(block, axis, distance):
    devices = range(lax.axis_size(axis))
    route = [(i - distance, i) for i in devices if i - distance in devices]
    return lax.ppermute(block, axis, route)


def doc_index(position, doc_starts):
    return jnp.sum((doc_starts[None, :] <= position[:, None]).astype(jnp.int32), axis=1) - 1


def collect(key_part, value_part, head_index):
    current_keys, current_values = (key_part, value_part)
    for bit in range(GROUP.bit_length() - 1):
        other_keys, other_values = from_partner((current_keys, current_values), "head", bit)
        is_lower = head_index // (1 << bit) % 2 == 0
        current_keys = jnp.where(
            is_lower,
            jnp.concatenate([current_keys, other_keys], axis=1),
            jnp.concatenate([other_keys, current_keys], axis=1),
        )
        current_values = jnp.where(
            is_lower,
            jnp.concatenate([current_values, other_values], axis=1),
            jnp.concatenate([other_values, current_values], axis=1),
        )
    return (current_keys, current_values)


def on_device(queries, keys, values, out_weight, doc_starts):
    rows_here = queries.shape[0]
    head_dim = queries.shape[1]
    earlier = WINDOW // rows_here
    block_rows = min(512, rows_here)
    scale = head_dim ** (-0.5)
    ctx_index = lax.axis_index("ctx")
    head_index = lax.axis_index("head")
    own_keys, own_values = collect(keys, values, head_index)
    key_list, value_list = ([], [])
    for distance in range(earlier, 0, -1):
        moved_keys, moved_values = shifted((own_keys, own_values), "ctx", distance)
        key_list.append(moved_keys)
        value_list.append(moved_values)
    keys_all = jnp.concatenate(key_list + [own_keys], axis=0)
    values_all = jnp.concatenate(value_list + [own_values], axis=0)
    base = ctx_index * rows_here
    key_positions = base - WINDOW + jnp.arange(WINDOW + rows_here, dtype=jnp.int32)
    key_docs = doc_index(key_positions, doc_starts)
    outputs = []
    for index in range(rows_here // block_rows):
        start = index * block_rows
        query_block = queries[start : start + block_rows]
        key_block = keys_all[start : start + block_rows + WINDOW]
        value_block = values_all[start : start + block_rows + WINDOW]
        query_pos = key_positions[WINDOW + start : WINDOW + start + block_rows]
        query_docs = key_docs[WINDOW + start : WINDOW + start + block_rows]
        block_pos = key_positions[start : start + block_rows + WINDOW]
        block_docs = key_docs[start : start + block_rows + WINDOW]
        allowed = (block_pos[None, :] >= 0) & (block_pos[None, :] <= query_pos[:, None])
        allowed = allowed & (block_pos[None, :] > query_pos[:, None] - WINDOW)
        allowed = allowed & (block_docs[None, :] == query_docs[:, None])
        scores = (
            lax.dot_general(
                query_block, key_block, (((1,), (1,)), ((), ())), preferred_element_type=jnp.float32
            )
            * scale
        )
        scores = jnp.where(allowed, scores, -1e30)
        row_max = jnp.max(scores, axis=1, keepdims=True)
        weights = jnp.where(allowed, jnp.exp(scores - row_max), 0.0)
        totals = jnp.sum(weights, axis=1, keepdims=True)
        summed = jnp.dot(
            weights.astype(jnp.bfloat16), value_block, preferred_element_type=jnp.float32
        )
        outputs.append((summed / totals).astype(jnp.bfloat16))
    attention = jnp.concatenate(outputs, axis=0)
    return lax.psum_scatter(
        jnp.dot(attention, out_weight, preferred_element_type=jnp.float32).astype(jnp.bfloat16),
        "head",
        scatter_dimension=0,
        tiled=True,
    )


def solution(mesh):
    placed = (P("ctx", "head"), P("ctx", "head"), P("ctx", "head"), P("head", None), P())
    return jax.shard_map(
        on_device, mesh=mesh, in_specs=placed, out_specs=P(("ctx", "head"), None), check_vma=False
    )
```

profile of v0, /device:TPU:97, one launch (start us, length us, event | category | flops | bytes accessed | tf_op | source)
XLA Modules:
  0.0 279.6 jit_solution(5876032834061386195)
XLA Ops:
  6.5 0.0 copy-start
  6.5 0.0 reduce-scatter.2.cloned.1.call-start
  6.5 0.7 collective-permute-start
  7.2 0.0 collective-permute-start.4
  7.2 0.8 convert_reduce_fusion
  8.1 0.3 collective-permute-done
  8.4 1.0 maximum_select_fusion.2
  9.5 1.4 collective-permute-start.1
  10.8 0.0 collective-permute-done.4
  10.8 1.0 maximum_select_fusion.3
  11.9 0.3 collective-permute-start.5
  12.1 4.9 %collective-permute-done.1 = bf16[2048,64]{0,1:T(8,128)(2,1)S(1)} collective-permute-done((bf16[2048,64]{0,1:T(8,128)(2,1)S(1)}, bf16[2048,64]{0,1:T(8,128)(2,1)S(1)}, u32[]{:S(2)}, u32[]{:S(2)}) %collective-permute-start.1) | collective-permute-done | bytes 262176 | tf_op jit(solution)/shard_map/ppermute | solution.py:13
  17.1 0.1 maximum_select_fusion
  17.2 4.8 %collective-permute-start.3 = (bf16[2048,128]{0,1:T(8,128)(2,1)S(1)}, bf16[2048,128]{0,1:T(8,128)(2,1)S(1)}, u32[]{:S(2)}, u32[]{:S(2)}) collective-permute-start(bf16[2048,128]{0,1:T(8,128)(2,1)S(1)} %maximum_select_fusion), channel_id=1, source_target_pairs={{0,32},{32,64},{64,96},{96,128},{128,160},{160,192},{192,224},{1,3... | collective-permute-start | bytes 1572872 | tf_op jit(solution)/shard_map/ppermute | solution.py:19
  21.9 3.1 %collective-permute-start.2 = (bf16[2048,128]{0,1:T(8,128)(2,1)S(1)}, bf16[2048,128]{0,1:T(8,128)(2,1)S(1)}, u32[]{:S(2)}, u32[]{:S(2)}) collective-permute-start(bf16[2048,128]{0,1:T(8,128)(2,1)S(1)} %maximum_select_fusion), channel_id=1, source_target_pairs={{0,64},{32,96},{64,128},{96,160},{128,192},{160,224},{1,65},{33,97... | collective-permute-start | bytes 1572872 | tf_op jit(solution)/shard_map/ppermute | solution.py:19
  25.1 0.0 collective-permute-done.5
  25.1 0.1 maximum_select_fusion.1
  25.2 2.6 collective-permute-start.7
  27.9 3.0 %collective-permute-start.6 = (bf16[2048,128]{0,1:T(8,128)(2,1)S(1)}, bf16[2048,128]{0,1:T(8,128)(2,1)S(1)}, u32[]{:S(2)}, u32[]{:S(2)}) collective-permute-start(bf16[2048,128]{0,1:T(8,128)(2,1)S(1)} %maximum_select_fusion.1), channel_id=1, source_target_pairs={{0,64},{32,96},{64,128},{96,160},{128,192},{160,224},{1,65},{33,97... | collective-permute-start | bytes 1572872 | tf_op jit(solution)/shard_map/ppermute | solution.py:19
  30.8 1.0 collective-permute-done.3
  31.8 21.2 %collective-permute-done.2 = bf16[2048,128]{0,1:T(8,128)(2,1)S(1)} collective-permute-done((bf16[2048,128]{0,1:T(8,128)(2,1)S(1)}, bf16[2048,128]{0,1:T(8,128)(2,1)S(1)}, u32[]{:S(2)}, u32[]{:S(2)}) %collective-permute-start.2) | collective-permute-done | bytes 524320 | tf_op jit(solution)/shard_map/ppermute | solution.py:19
  53.0 0.1 pad_maximum_fusion
  53.2 0.0 copy-start.1
  53.2 6.0 %fusion.3 = (f32[512]{0:T(512)S(1)}, f32[4608,512]{1,0:T(8,128)S(1)}) fusion(s32[512]{0:T(512)S(1)} %get-tuple-element.26, s32[4608]{0:T(1024)S(1)} %get-tuple-element.22, s32[512]{0:T(512)S(1)} %get-tuple-element.17, s32[512]{0:T(512)S(1)} %get-tuple-element.18, s32[4608]{0:T(1024)S(1)} %get-tuple-element.10, pred[4608]{0:T(1024)(128)(4,1)S(1)} %get-tuple-element.8, ...), kind=kOutput, calls=%fused_computation.16 | convolution fusion | flops 625212928 | bytes 10802176 | tf_op jit(solution)/shard_map/dot_general | solution.py:77
  59.1 0.0 copy-done.1
  59.2 5.0 %fusion.2 = (f32[512]{0:T(512)S(1)}, f32[4608,512]{1,0:T(8,128)S(1)}) fusion(s32[512]{0:T(512)S(1)} %get-tuple-element.27, s32[4608]{0:T(1024)S(1)} %get-tuple-element.23, s32[512]{0:T(512)S(1)} %get-tuple-element.16, s32[512]{0:T(512)S(1)} %get-tuple-element.19, s32[4608]{0:T(1024)S(1)} %get-tuple-element.11, pred[4608]{0:T(1024)(128)(4,1)S(1)} %get-tuple-element.7, ...), kind=kOutput, calls=%fused_computation.15 | convolution fusion | flops 625212928 | bytes 10802176 | tf_op jit(solution)/shard_map/dot_general | solution.py:77
  64.1 13.1 %fusion.8 = (f32[512]{0:T(512)S(1)}, f32[512]{0:T(512)S(1)}) fusion(f32[4608,512]{1,0:T(8,128)S(1)} %get-tuple-element.32, f32[512]{0:T(512)S(1)} %get-tuple-element.31, s32[512]{0:T(512)S(1)} %get-tuple-element.27, s32[4608]{0:T(1024)S(1)} %get-tuple-element.23, s32[512]{0:T(512)S(1)} %get-tuple-element.16, s32[512]{0:T(512)S(1)} %get-tuple-element.19, ...), kind=kLoop, calls=%fused_computation.21 | loop fusion | flops 51903488 | bytes 18977792 | tf_op jit(solution)/shard_map/reduce_sum | solution.py:85
  77.3 0.0 collective-permute-done.7
  77.3 9.7 %collective-permute-done.6 = bf16[2048,128]{0,1:T(8,128)(2,1)S(1)} collective-permute-done((bf16[2048,128]{0,1:T(8,128)(2,1)S(1)}, bf16[2048,128]{0,1:T(8,128)(2,1)S(1)}, u32[]{:S(2)}, u32[]{:S(2)}) %collective-permute-start.6) | collective-permute-done | bytes 524320 | tf_op jit(solution)/shard_map/ppermute | solution.py:19
  87.0 0.1 pad_maximum_fusion.1
  87.1 6.1 %fusion.67 = bf16[512,128]{1,0:T(8,128)(2,1)S(1)} fusion(bf16[6144,128]{0,1:T(8,128)(2,1)S(1)} %pad_maximum_fusion.1, f32[4608,512]{1,0:T(8,128)S(1)} %get-tuple-element.30, f32[512]{0:T(512)S(1)} %get-tuple-element.29, f32[512]{0:T(512)S(1)} %get-tuple-element.40, s32[512]{0:T(512)S(1)} %get-tuple-element.26, s32[512]{0:T(512)S(1)} %get-tuple-element.17, ...), kind=kOutput, calls=%fused_computation.50 | convolution fusion | flops 630063104 | bytes 10804224 | tf_op jit(solution)/shard_map/dot_general | solution.py:86
  93.2 6.0 %fusion.57 = bf16[512,128]{1,0:T(8,128)(2,1)S(1)} fusion(bf16[6144,128]{0,1:T(8,128)(2,1)S(1)} %pad_maximum_fusion.1, f32[4608,512]{1,0:T(8,128)S(1)} %get-tuple-element.32, f32[512]{0:T(512)S(1)} %get-tuple-element.31, f32[512]{0:T(512)S(1)} %get-tuple-element.39, s32[512]{0:T(512)S(1)} %get-tuple-element.27, s32[512]{0:T(512)S(1)} %get-tuple-element.16, ...), kind=kOutput, calls=%fused_computation.48 | convolution fusion | flops 630063104 | bytes 10804224 | tf_op jit(solution)/shard_map/dot_general | solution.py:86
  99.3 5.4 %fusion.1 = (f32[512]{0:T(512)S(1)}, f32[4608,512]{1,0:T(8,128)S(1)}) fusion(s32[512]{0:T(512)S(1)} %get-tuple-element.28, s32[4608]{0:T(1024)S(1)} %get-tuple-element.24, s32[512]{0:T(512)S(1)} %get-tuple-element.15, s32[512]{0:T(512)S(1)} %get-tuple-element.20, s32[4608]{0:T(1024)S(1)} %get-tuple-element.12, pred[4608]{0:T(1024)(128)(4,1)S(1)} %get-tuple-element.6, ...), kind=kOutput, calls=%fused_computation.14 | convolution fusion | flops 625212928 | bytes 10802176 | tf_op jit(solution)/shard_map/dot_general | solution.py:77
  104.7 5.0 %fusion = (f32[512]{0:T(512)S(1)}, f32[4608,512]{1,0:T(8,128)S(1)}) fusion(s32[512]{0:T(512)S(1)} %get-tuple-element.25, s32[4608]{0:T(1024)S(1)} %get-tuple-element.21, s32[512]{0:T(512)S(1)} %get-tuple-element.14, s32[512]{0:T(512)S(1)} %get-tuple-element.13, s32[4608]{0:T(1024)S(1)} %get-tuple-element.9, pred[4608]{0:T(1024)(128)(4,1)S(1)} %get-tuple-element.5, ...), kind=kOutput, calls=%fused_computation.13 | convolution fusion | flops 625212928 | bytes 10802176 | tf_op jit(solution)/shard_map/dot_general | solution.py:77
  109.7 13.1 %fusion.4 = (f32[512]{0:T(512)S(1)}, f32[512]{0:T(512)S(1)}) fusion(f32[4608,512]{1,0:T(8,128)S(1)} %get-tuple-element.36, f32[512]{0:T(512)S(1)} %get-tuple-element.35, s32[512]{0:T(512)S(1)} %get-tuple-element.25, s32[4608]{0:T(1024)S(1)} %get-tuple-element.21, s32[512]{0:T(512)S(1)} %get-tuple-element.14, s32[512]{0:T(512)S(1)} %get-tuple-element.13, ...), kind=kLoop, calls=%fused_computation.17 | loop fusion | flops 51903488 | bytes 18977792 | tf_op jit(solution)/shard_map/reduce_sum | solution.py:85
  122.8 6.1 %fusion.47 = bf16[512,128]{1,0:T(8,128)(2,1)S(1)} fusion(bf16[6144,128]{0,1:T(8,128)(2,1)S(1)} %pad_maximum_fusion.1, f32[4608,512]{1,0:T(8,128)S(1)} %get-tuple-element.34, f32[512]{0:T(512)S(1)} %get-tuple-element.33, f32[512]{0:T(512)S(1)} %get-tuple-element.38, s32[512]{0:T(512)S(1)} %get-tuple-element.28, s32[512]{0:T(512)S(1)} %get-tuple-element.15, ...), kind=kOutput, calls=%fused_computation.46 | convolution fusion | flops 630063104 | bytes 10804224 | tf_op jit(solution)/shard_map/dot_general | solution.py:86
  128.9 6.0 %fusion.37 = bf16[512,128]{1,0:T(8,128)(2,1)S(1)} fusion(bf16[6144,128]{0,1:T(8,128)(2,1)S(1)} %pad_maximum_fusion.1, f32[4608,512]{1,0:T(8,128)S(1)} %get-tuple-element.36, f32[512]{0:T(512)S(1)} %get-tuple-element.35, f32[512]{0:T(512)S(1)} %get-tuple-element.37, s32[512]{0:T(512)S(1)} %get-tuple-element.25, s32[512]{0:T(512)S(1)} %get-tuple-element.14, ...), kind=kOutput, calls=%fused_computation.44 | convolution fusion | flops 630063104 | bytes 10804224 | tf_op jit(solution)/shard_map/dot_general | solution.py:86
  134.9 0.0 copy-done
  134.9 10.6 %convolution_convert_fusion = bf16[2048,4096]{1,0:T(8,128)(2,1)} fusion(bf16[128,4096]{1,0:T(8,128)(2,1)S(1)} %copy-done, bf16[512,128]{1,0:T(8,128)(2,1)S(1)} %fusion.67, bf16[512,128]{1,0:T(8,128)(2,1)S(1)} %fusion.57, bf16[512,128]{1,0:T(8,128)(2,1)S(1)} %fusion.47, bf16[512,128]{1,0:T(8,128)(2,1)S(1)} %fusion.37), kind=kOutput, calls=%fused_computation | convolution fusion | flops 2157969408 | bytes 18350080 | tf_op jit(solution)/shard_map/dot_general | solution.py:92
  145.5 0.0 reduce-scatter.2.cloned.1.call-update
  145.6 127.0 %reduce-scatter.2.cloned.1.call-done = bf16[64,4096]{1,0:T(8,128)(2,1)} async-done(((bf16[2048,4096]{1,0:T(8,128)(2,1)}), bf16[64,4096]{1,0:T(8,128)(2,1)}) %reduce-scatter.2.cloned.1.call-update) | async-done | bytes 524304 | tf_op jit(solution)/shard_map/reduce_scatter | solution.py:91
  (7 shorter events, 0.1 us)
Async XLA Ops:
  6.5 128.4 %copy-start = (bf16[128,4096]{1,0:T(8,128)(2,1)S(1)}, bf16[128,4096]{1,0:T(8,128)(2,1)}, u32[]{:S(2)}) copy-start(bf16[128,4096]{1,0:T(8,128)(2,1)} %param.8) | copy-start | bytes 3145732
  6.5 266.0 %reduce-scatter.2.cloned.1.call-start = ((), (), s32[]{:S(2)}) async-start(), calls=%async_computation.1 | async-start | bytes 17301504 | tf_op jit(solution)/shard_map/reduce_scatter | solution.py:91
  6.5 1.9 collective-permute-start
  7.2 3.6 %collective-permute-start.4 = (bf16[2048,32]{0,1:T(8,128)(2,1)}, bf16[2048,32]{0,1:T(8,128)(2,1)S(1)}, u32[]{:S(2)}, u32[]{:S(2)}) collective-permute-start(bf16[2048,32]{0,1:T(8,128)(2,1)} %param.7), channel_id=1, source_target_pairs={{0,1},{1,0},{2,3},{3,2},{4,5},{5,4},{6,7},{7,6},{8,9},{9,8},{10,11... | collective-permute-start | bytes 393224 | tf_op jit(solution)/shard_map/ppermute | solution.py:13
  9.5 7.6 %collective-permute-start.1 = (bf16[2048,64]{0,1:T(8,128)(2,1)S(1)}, bf16[2048,64]{0,1:T(8,128)(2,1)S(1)}, u32[]{:S(2)}, u32[]{:S(2)}) collective-permute-start(bf16[2048,64]{0,1:T(8,128)(2,1)S(1)} %maximum_select_fusion.2), channel_id=1, source_target_pairs={{0,2},{1,3},{2,0},{3,1},{4,6},{5,7},{6,4},{7,5},{8,10},{9,11},{10,... | collective-permute-start | bytes 786440 | tf_op jit(solution)/shard_map/ppermute | solution.py:13
  11.9 13.2 %collective-permute-start.5 = (bf16[2048,64]{0,1:T(8,128)(2,1)S(1)}, bf16[2048,64]{0,1:T(8,128)(2,1)S(1)}, u32[]{:S(2)}, u32[]{:S(2)}) collective-permute-start(bf16[2048,64]{0,1:T(8,128)(2,1)S(1)} %maximum_select_fusion.3), channel_id=1, source_target_pairs={{0,2},{1,3},{2,0},{3,1},{4,6},{5,7},{6,4},{7,5},{8,10},{9,11},{10,... | collective-permute-start | bytes 786440 | tf_op jit(solution)/shard_map/ppermute | solution.py:13
  17.2 14.6 %collective-permute-start.3 = (bf16[2048,128]{0,1:T(8,128)(2,1)S(1)}, bf16[2048,128]{0,1:T(8,128)(2,1)S(1)}, u32[]{:S(2)}, u32[]{:S(2)}) collective-permute-start(bf16[2048,128]{0,1:T(8,128)(2,1)S(1)} %maximum_select_fusion), channel_id=1, source_target_pairs={{0,32},{32,64},{64,96},{96,128},{128,160},{160,192},{192,224},{1,3... | collective-permute-start | bytes 1572872 | tf_op jit(solution)/shard_map/ppermute | solution.py:19
  21.9 31.1 %collective-permute-start.2 = (bf16[2048,128]{0,1:T(8,128)(2,1)S(1)}, bf16[2048,128]{0,1:T(8,128)(2,1)S(1)}, u32[]{:S(2)}, u32[]{:S(2)}) collective-permute-start(bf16[2048,128]{0,1:T(8,128)(2,1)S(1)} %maximum_select_fusion), channel_id=1, source_target_pairs={{0,64},{32,96},{64,128},{96,160},{128,192},{160,224},{1,65},{33,97... | collective-permute-start | bytes 1572872 | tf_op jit(solution)/shard_map/ppermute | solution.py:19
  25.2 52.1 %collective-permute-start.7 = (bf16[2048,128]{0,1:T(8,128)(2,1)S(1)}, bf16[2048,128]{0,1:T(8,128)(2,1)S(1)}, u32[]{:S(2)}, u32[]{:S(2)}) collective-permute-start(bf16[2048,128]{0,1:T(8,128)(2,1)S(1)} %maximum_select_fusion.1), channel_id=1, source_target_pairs={{0,32},{32,64},{64,96},{96,128},{128,160},{160,192},{192,224},{1,3... | collective-permute-start | bytes 1572872 | tf_op jit(solution)/shard_map/ppermute | solution.py:19
  27.9 59.1 %collective-permute-start.6 = (bf16[2048,128]{0,1:T(8,128)(2,1)S(1)}, bf16[2048,128]{0,1:T(8,128)(2,1)S(1)}, u32[]{:S(2)}, u32[]{:S(2)}) collective-permute-start(bf16[2048,128]{0,1:T(8,128)(2,1)S(1)} %maximum_select_fusion.1), channel_id=1, source_target_pairs={{0,64},{32,96},{64,128},{96,160},{128,192},{160,224},{1,65},{33,97... | collective-permute-start | bytes 1572872 | tf_op jit(solution)/shard_map/ppermute | solution.py:19
  53.2 6.0 %copy-start.1 = (bf16[2048,128]{1,0:T(8,128)(2,1)S(1)}, bf16[2048,128]{1,0:T(8,128)(2,1)}, u32[]{:S(2)}) copy-start(bf16[2048,128]{1,0:T(8,128)(2,1)} %param.5) | copy-start | bytes 1572868
Sparse Core Ops, SparseCore 0:
  145.7 126.8 reduce-scatter.1
where the time goes:
time: 285 us; the launch traced here: 280 us
  waiting for transfers between devices  164 us (58%)
  matrix products  56.2 us (20%)
  other arithmetic  29.6 us (10%)
  starting transfers between devices  15.8 us (6%)
  between operations  13.8 us (5%)
    reduce_scatter x1, waiting for transfers between devices, on_device(): lax.psum_scatter(jnp.dot(attention, out_weight, preferred_element_type=jn...  127 us
    ppermute x4, waiting for transfers between devices, shifted(): return lax.ppermute(block, axis, route)  31.8 us
    reduce_sum x2, other arithmetic, on_device(): totals = jnp.sum(weights, axis=1, keepdims=True)  26.2 us
    dot_general x4, matrix products, on_device(): jnp.dot(weights.astype(jnp.bfloat16), value_block, preferred_element_type...  24.3 us
    dot_general x4, matrix products, on_device(): lax.dot_general(query_block, key_block, (((1,), (1,)), ((), ())), preferr...  21.3 us
    ppermute x4, starting transfers between devices, shifted(): return lax.ppermute(block, axis, route)  13.5 us
    dot_general x1, matrix products, on_device(): jnp.dot(attention, out_weight, preferred_element_type=jnp.float32)  10.6 us
  transfers between devices with their start and end apart: 9, of which 6 were waited for; matrix products, arithmetic and copies ran while one was open for 10% of the time, Pallas kernels for 0%

commit v1 on v0

v1 whole, which is shorter than its diff:
```python
import jax
import jax.numpy as jnp
from jax import lax
from jax.experimental import pallas as pl
from jax.experimental.pallas import tpu as pltpu
from jax.sharding import PartitionSpec as P

GROUP = 4
WINDOW = 4096
T = 2048
HD = 128
D = 4096
DOCS = 16
Z, X, Y = 8, 4, 4
HALF = D // 2
NC = 4
CW = HALF // NC
QT = T // X
SUB = QT // Y
TQ = 512
TK = 1024
NEG = -1e30
SCALE = 1.4426950408889634 * HD**-0.5

KV_Z, KV_Y, KV_CA, KV_CB = 0, 3, 6, 9
W_UP, W_DOWN, W_FUP, W_FDOWN, W_SIB = 12, 20, 28, 32, 36
A_X, A_SIB = 37, 40
R_UP, R_DOWN, M_UP, M_DOWN, S_UP, S_DOWN, F_SIB = 44, 48, 52, 56, 60, 64, 68
N_COPIES = 72
L_W, L_ATT, L_OUT = 0, 1, 2
N_LOCAL = 6


def kernel(
    starts_ref, q_ref, k_ref, v_ref, w_ref, out_ref,
    kv, kn, q2, lo_ref, m_ref, acc, obuf, att, wb, part, rel, rin, msg, min_, res,
    ssem, rsem, lsem,
):
    z = lax.axis_index("ctx")
    head = lax.axis_index("head")
    c = lax.rem(head, 2)
    y = lax.rem(head // 2, Y)
    x = head // (2 * Y)
    r = lax.rem(head, GROUP)

    def at(zz, xx, yy, cc):
        return (zz, (xx * Y + yy) * 2 + cc)

    def xx(step):
        return lax.rem(x + step, X)

    def yy(step):
        return lax.rem(y + step, Y)

    z_next = at(lax.rem(z + 1, Z), x, y, c)
    z_prev = at(lax.rem(z + Z - 1, Z), x, y, c)
    sibling = at(z, x, y, 1 - c)
    y_up, y_down = at(z, x, yy(1), c), at(z, x, yy(3), c)
    y_pair = at(z, x, y + 1 - 2 * lax.rem(y, 2), c)

    def copy(src, dst, device, send, recv):
        return pltpu.make_async_remote_copy(
            src_ref=src,
            dst_ref=dst,
            send_sem=ssem.at[send],
            recv_sem=rsem.at[recv],
            device_id=device,
            device_id_type=pl.DeviceIdType.MESH,
        )

    sent = []

    def send(src, dst, device, index, recv=None):
        one = copy(src, dst, device, index, index if recv is None else recv)
        one.start()
        sent.append(one)

    def arrived(dst, index):
        copy(dst, dst, sibling, 0, index).wait_recv()

    def piece(block, member):
        return kv.at[block, :, pl.ds(pl.multiple_of(32 * member, 32), 32), :]

    def w_rows(source_x, source_c):
        return pl.ds(pl.multiple_of(HD * (2 * source_x + source_c), HD), HD)

    def col(start, width):
        return pl.ds(pl.multiple_of(start, 128), width)

    partners = [z_next, z_prev, sibling, y_up, y_down]
    partners += [at(z, xx(1), y, 0), at(z, xx(1), y, 1), at(z, xx(3), y, 0), at(z, xx(3), y, 1)]
    partners += [at(z, xx(2), y, c)]
    barrier = pltpu.get_barrier_semaphore()
    for device in partners:
        pl.semaphore_signal(barrier, inc=1, device_id=device, device_id_type=pl.DeviceIdType.MESH)
    own = pl.ds(pl.multiple_of(32 * r, 32), 32)
    kv[0, 0, own, :] = k_ref[...]
    kv[0, 1, own, :] = v_ref[...]
    pl.semaphore_wait(barrier, len(partners))

    send(piece(0, r), piece(0, r), y_pair, KV_Y)
    send(piece(0, r), piece(1, r), z_next, KV_Z)
    send(piece(0, r), piece(0, r), sibling, KV_CA)
    for k in range(NC):
        for half in range(2):
            src = w_ref.at[:, pl.ds(half * HALF + k * CW, CW)]
            dst = wb.at[w_rows(x, c), pl.ds(k * CW, CW)]
            send(src, dst, at(z, xx(1), y, half), W_UP + 2 * k + half, W_UP + 2 * k + c)
            send(src, dst, at(z, xx(3), y, half), W_DOWN + 2 * k + half, W_DOWN + 2 * k + c)
    send(w_ref.at[:, col((1 - c) * HALF, HALF)], wb.at[w_rows(x, c), :], sibling, W_SIB)
    w_local = pltpu.make_async_copy(
        w_ref.at[:, col(c * HALF, HALF)], wb.at[w_rows(x, c), :], lsem.at[L_W]
    )
    w_local.start()

    def forward_w(k):
        for source_c in range(2):
            arrived(wb.at[w_rows(xx(3), source_c), pl.ds(k * CW, CW)], W_UP + 2 * k + source_c)
        for source_c in range(2):
            arrived(wb.at[w_rows(xx(1), source_c), pl.ds(k * CW, CW)], W_DOWN + 2 * k + source_c)
        below = wb.at[pl.ds(pl.multiple_of(2 * HD * xx(3), 2 * HD), 2 * HD), pl.ds(k * CW, CW // 2)]
        above = wb.at[
            pl.ds(pl.multiple_of(2 * HD * xx(1), 2 * HD), 2 * HD), pl.ds(k * CW + CW // 2, CW // 2)
        ]
        send(below, below, at(z, xx(1), y, c), W_FUP + k)
        send(above, above, at(z, xx(3), y, c), W_FDOWN + k)

    scaled = q_ref[...].astype(jnp.float32).T * SCALE
    coarse = scaled.astype(jnp.bfloat16)
    q2[:HD] = coarse
    q2[HD:] = (scaled - coarse.astype(jnp.float32)).astype(jnp.bfloat16)
    base = z * T
    local = lax.broadcasted_iota(jnp.int32, (8, T), 1)
    begin = jnp.zeros((8, T), jnp.int32)
    for d in range(DOCS):
        start = starts_ref[d]
        begin = jnp.where(local + base >= start, start, begin)
    lo_ref[...] = jnp.maximum(begin - base + WINDOW, local + 1)

    def scores(block, offset, k0, q0, n_sub, width, diagonal):
        keys = kn[block, pl.ds(k0, TK), :]
        keys = jnp.concatenate([keys, keys], axis=1)
        values = jnp.concatenate(
            [kv[block, 1, :, pl.ds(k0, TK)], jnp.ones((16, TK), jnp.bfloat16)], axis=0
        )
        tiles = []
        for u in range(n_sub):
            columns = pl.ds(q0 + u * width, width)
            tiles.append(jnp.dot(keys, q2[:, columns], preferred_element_type=jnp.float32))
        for u in range(n_sub):
            columns = pl.ds(q0 + u * width, width)
            place = lax.broadcasted_iota(jnp.int32, (TK, width), 0)
            allowed = place >= lo_ref[:1, columns] - (offset + k0)
            if diagonal:
                query = lax.broadcasted_iota(jnp.int32, (1, width), 1) + (q0 + u * width - k0)
                allowed &= place <= query
            tile = jnp.where(allowed, tiles[u], NEG)
            top = jnp.max(tile, axis=0, keepdims=True)
            if not diagonal:
                before = m_ref[:1, columns]
                top = jnp.maximum(before, top)
                keep = jnp.exp2(before - top)
            weights = jnp.exp2(tile - top).astype(jnp.bfloat16)
            added = jnp.dot(values, weights, preferred_element_type=jnp.float32)
            m_ref[:1, columns] = top
            acc[:, columns] = added if diagonal else acc[:, columns] * keep + added

    arrived(piece(0, r ^ 2), KV_Y)
    send(piece(0, r ^ 2), piece(0, r ^ 2), sibling, KV_CB)
    arrived(piece(1, r), KV_Z)
    send(piece(1, r), piece(1, r), y_pair, KV_Y + 1)
    send(piece(1, r), piece(2, r), z_next, KV_Z + 1)
    send(piece(1, r), piece(1, r), sibling, KV_CA + 1)
    arrived(piece(0, r ^ 1), KV_CA)
    arrived(piece(0, r ^ 3), KV_CB)
    kn[0] = kv[0, 0].T

    @pl.loop(0, T // TK)
    def _(i):
        q0 = pl.multiple_of(i * TK, TK)
        scores(0, WINDOW, q0, q0, TK // TQ, TQ, True)

        @pl.loop(0, i)
        def _(k):
            scores(0, WINDOW, pl.multiple_of(k * TK, TK), q0, TK // TQ, TQ, False)

    arrived(piece(2, r), KV_Z + 1)
    send(piece(2, r), piece(2, r), y_pair, KV_Y + 2)
    send(piece(2, r), piece(2, r), sibling, KV_CA + 2)
    arrived(piece(1, r ^ 2), KV_Y + 1)
    send(piece(1, r ^ 2), piece(1, r ^ 2), sibling, KV_CB + 1)
    forward_w(0)
    arrived(piece(1, r ^ 1), KV_CA + 1)
    arrived(piece(1, r ^ 3), KV_CB + 1)
    kn[1] = kv[1, 0].T

    for i in range(T // TK):

        @pl.loop(0, T // TK)
        def _(k):
            scores(1, T, pl.multiple_of(k * TK, TK), i * TK, TK // TQ, TQ, False)

        forward_w(1 + i)
        if i == 0:
            arrived(piece(2, r ^ 2), KV_Y + 2)
            send(piece(2, r ^ 2), piece(2, r ^ 2), sibling, KV_CB + 2)

    arrived(piece(2, r ^ 1), KV_CA + 2)
    arrived(piece(2, r ^ 3), KV_CB + 2)
    kn[2] = kv[2, 0].T

    att_own = att.at[:, w_rows(x, c)]
    for i, step in enumerate((2, 1, 3, 0)):
        quarter = xx(step)
        q0 = pl.multiple_of(quarter * QT, QT)

        @pl.loop(q0 // TK, T // TK)
        def _(k):
            scores(2, 0, pl.multiple_of(k * TK, TK), q0, 2, QT // 2, False)

        columns = pl.ds(q0, QT)
        total = acc[HD : HD + 1, columns]
        obuf[i] = (acc[:HD, columns] * (1.0 / total)).T.astype(jnp.bfloat16)
        if step:
            send(obuf.at[i], att_own, at(z, quarter, y, c), A_X + step - 1)
        else:
            send(obuf.at[i], att_own, sibling, A_SIB)
            att_local = pltpu.make_async_copy(obuf.at[i], att_own, lsem.at[L_ATT])
            att_local.start()
    forward_w(3)
    for step in (2, 1, 3):
        slot = att.at[:, w_rows(xx(4 - step), c)]
        arrived(slot, A_X + step - 1)
        send(slot, slot, sibling, A_SIB + step)
    arrived(att.at[:, w_rows(x, 1 - c)], A_SIB)
    for step in (2, 1, 3):
        arrived(att.at[:, w_rows(xx(4 - step), 1 - c)], A_SIB + step)
    att_local.wait()
    w_local.wait()
    arrived(wb.at[w_rows(x, 1 - c), :], W_SIB)

    left, right = pl.ds(0, CW // 2), pl.ds(CW // 2, CW // 2)

    def sub(k, block, half):
        return part[k, pl.ds(pl.multiple_of(block * SUB, SUB), SUB), half]

    def project(k):
        rows = pl.ds(pl.multiple_of(2 * HD * xx(2), 2 * HD), 2 * HD)
        arrived(wb.at[rows, pl.ds(k * CW, CW // 2)], W_FUP + k)
        arrived(wb.at[rows, pl.ds(k * CW + CW // 2, CW // 2)], W_FDOWN + k)
        part[k] = jnp.dot(
            att[...], wb[:, pl.ds(k * CW, CW)], preferred_element_type=jnp.float32
        )
        rel[k, 0] = sub(k, yy(2), left).astype(jnp.bfloat16)
        rel[k, 1] = sub(k, yy(2), right).astype(jnp.bfloat16)
        send(rel.at[k, 0], rin.at[k, 0], y_up, R_UP + k)
        send(rel.at[k, 1], rin.at[k, 1], y_down, R_DOWN + k)
        msg[k, 0] = sub(k, yy(1), right).astype(jnp.bfloat16)
        msg[k, 1] = sub(k, yy(3), left).astype(jnp.bfloat16)
        send(msg.at[k, 0], min_.at[k, 0], y_up, M_UP + k)
        send(msg.at[k, 1], min_.at[k, 1], y_down, M_DOWN + k)

    def relay(k):
        arrived(rin.at[k, 0], R_UP + k)
        msg[k, 2] = (sub(k, yy(1), left) + rin[k, 0].astype(jnp.float32)).astype(jnp.bfloat16)
        send(msg.at[k, 2], min_.at[k, 2], y_up, S_UP + k)
        arrived(rin.at[k, 1], R_DOWN + k)
        msg[k, 3] = (sub(k, yy(3), right) + rin[k, 1].astype(jnp.float32)).astype(jnp.bfloat16)
        send(msg.at[k, 3], min_.at[k, 3], y_down, S_DOWN + k)

    kept = []

    def finish(k):
        arrived(min_.at[k, 0], M_UP + k)
        arrived(min_.at[k, 1], M_DOWN + k)
        arrived(min_.at[k, 2], S_UP + k)
        arrived(min_.at[k, 3], S_DOWN + k)
        for half, columns, near, far in ((0, left, 1, 2), (1, right, 0, 3)):
            total = sub(k, y, columns) + min_[k, near].astype(jnp.float32)
            total += min_[k, far].astype(jnp.float32)
            res[k, :, columns] = total.astype(jnp.bfloat16)
        place = out_ref.at[:, col(c * HALF + k * CW, CW)]
        rows = SUB // 2
        one = pltpu.make_async_copy(
            res.at[k, pl.ds(pl.multiple_of(c * rows, rows), rows), :], place, lsem.at[L_OUT + k]
        )
        one.start()
        kept.append(one)
        send(
            res.at[k, pl.ds(pl.multiple_of((1 - c) * rows, rows), rows), :], place, sibling, F_SIB + k
        )

    for k in range(NC + 2):
        if k < NC:
            project(k)
        if 1 <= k <= NC:
            relay(k - 1)
        if k >= 2:
            finish(k - 2)
    for k in range(NC):
        arrived(out_ref.at[:, col((1 - c) * HALF + k * CW, CW)], F_SIB + k)
    for one in kept:
        one.wait()
    for one in sent:
        one.wait_send()


def on_device(queries, keys, values, out_weight, doc_starts):
    bf16, f32 = jnp.bfloat16, jnp.float32
    vmem = pl.BlockSpec(memory_space=pltpu.VMEM)
    return pl.pallas_call(
        kernel,
        out_shape=jax.ShapeDtypeStruct((SUB // 2, D), bf16),
        in_specs=[pl.BlockSpec(memory_space=pltpu.SMEM), vmem, vmem, vmem, vmem],
        out_specs=pl.BlockSpec(memory_space=pl.ANY),
        scratch_shapes=[
            pltpu.VMEM((3, 2, HD, T), bf16),
            pltpu.VMEM((3, T, HD), bf16),
            pltpu.VMEM((2 * HD, T), bf16),
            pltpu.VMEM((8, T), jnp.int32),
            pltpu.VMEM((8, T), f32),
            pltpu.VMEM((HD + 16, T), f32),
            pltpu.VMEM((X, QT, HD), bf16),
            pltpu.VMEM((QT, 2 * X * HD), bf16),
            pltpu.VMEM((2 * X * HD, HALF), bf16),
            pltpu.VMEM((NC, QT, CW), f32),
            pltpu.VMEM((NC, 2, SUB, CW // 2), bf16),
            pltpu.VMEM((NC, 2, SUB, CW // 2), bf16),
            pltpu.VMEM((NC, 4, SUB, CW // 2), bf16),
            pltpu.VMEM((NC, 4, SUB, CW // 2), bf16),
            pltpu.VMEM((NC, SUB, CW), bf16),
            pltpu.SemaphoreType.DMA((N_COPIES,)),
            pltpu.SemaphoreType.DMA((N_COPIES,)),
            pltpu.SemaphoreType.DMA((N_LOCAL,)),
        ],
        compiler_params=pltpu.CompilerParams(
            collective_id=0, has_side_effects=True, vmem_limit_bytes=56 * 2**20
        ),
    )(doc_starts, queries, keys.T, values.T, out_weight)


def solution(mesh):
    placed = (P("ctx", "head"), P("ctx", "head"), P("ctx", "head"), P("head", None), P())
    return jax.shard_map(
        on_device, mesh=mesh, in_specs=placed, out_specs=P(("ctx", "head"), None), check_vma=False
    )
```

time: 285 us -> 75.7 us (0.27)
  the two profiles are of different devices: /device:TPU:97 before, /device:TPU:1 now
where the time goes in v1:
time: 75.7 us; the launch traced here: 75.5 us
  Pallas kernels  73.6 us (97%)
  local copies, waits for them, and re-layouts  1.87 us (2%)
    pallas_call x1, Pallas kernels, on_device(): pl.pallas_call(kernel, out_shape=jax.ShapeDtypeStruct((SUB // 2, D), bf16...  73.6 us
    unnamed x1, local copies, waits for them, and re-layouts  1.87 us

profile of v1, /device:TPU:1, one launch (start us, length us, event | category | flops | bytes accessed | tf_op | source)
XLA Modules:
  0.0 75.5 jit_solution(13311296175257341310)
XLA Ops:
  0.0 73.6 %shard_map.55 = bf16[64,4096]{1,0:T(8,128)(2,1)} custom-call(s32[16]{0:T(128)} %starts_ref.1, bf16[2048,128]{1,0:T(8,128)(2,1)} %q_ref.1, bf16[32,2048]{1,0:T(8,128)(2,1)} %bitcast.2, bf16[32,2048]{1,0:T(8,128)(2,1)} %bitcast.3, bf16[128,4096]{1,0:T(8,128)(2,1)} %w_ref.1), custom_call_target="tpu_custom_call" | custom-call | tf_op jit(solution)/shard_map/pallas_call | solution.py:311
  73.6 1.9 %copy.7 = bf16[64,4096]{1,0:T(8,128)(2,1)} copy(bf16[64,4096]{1,0:T(8,128)(2,1)} %shard_map.55) | data formatting | bytes 1048576

commit v2 on v1

v2 whole, which is shorter than its diff:
```python
import jax
import jax.numpy as jnp
from jax import lax
from jax.experimental import pallas as pl
from jax.experimental.pallas import tpu as pltpu
from jax.sharding import PartitionSpec as P

GROUP = 4
WINDOW = 4096
T = 2048
HD = 128
D = 4096
DOCS = 16
Z, X, Y = 8, 4, 4
HALF = D // 2
PATH = HALF // 2
CW = 512
NC = PATH // CW
QT = T // X
SUB = QT // Y
TQ = 512
TK = 1024
NEG = -1e30
SCALE = 1.4426950408889634 * HD**-0.5

KV_Y0, KV_Y1, KV_Y2, KV_Z1, KV_Z2A, KV_Z2B = 0, 2, 4, 5, 7, 9
KV_CA, KV_CB, KV_CB2 = 10, 13, 15
W_UP, W_DOWN, W_FUP, W_FDOWN, W_SIB = 17, 21, 25, 27, 29
V_IN, V_OUT, V_FIN, V_FOUT, V_ZUP, V_ZDOWN = 31, 33, 35, 36, 37, 40
A_X, A_Y, A_XSIB, A_YSIB = 43, 46, 58, 62
R_UP = 66
N_COPIES = R_UP + 7 * 2 * NC
L_W, L_ATT, L_OUT = 0, 2, 7
N_LOCAL = L_OUT + 2 * NC


def kernel(
    starts_ref, q_ref, k_ref, v_ref, w_ref, out_ref,
    kv, kn, q2, lo_ref, m_ref, acc, obuf, att, wb, part, rel, rin, msg, min_, res,
    ssem, rsem, lsem,
):
    z = lax.axis_index("ctx")
    head = lax.axis_index("head")
    c = lax.rem(head, 2)
    y = lax.rem(head // 2, Y)
    x = head // (2 * Y)
    r = lax.rem(head, GROUP)
    odd_y, odd_z = lax.rem(y, 2), lax.rem(z, 2)

    def at(z_, x_, y_, c_):
        return (z_, (x_ * Y + y_) * 2 + c_)

    def xx(step):
        return lax.rem(x + step, X)

    def yy(step):
        return lax.rem(y + step, Y)

    z_next = at(lax.rem(z + 1, Z), x, y, c)
    z_prev = at(lax.rem(z + Z - 1, Z), x, y, c)
    sibling = at(z, x, y, 1 - c)
    inner = yy(1 + 2 * odd_y)
    outer = yy(3 - 2 * odd_y)
    y_pair = at(z, x, inner, c)

    def copy(src, dst, device, send, recv):
        return pltpu.make_async_remote_copy(
            src_ref=src,
            dst_ref=dst,
            send_sem=ssem.at[send],
            recv_sem=rsem.at[recv],
            device_id=device,
            device_id_type=pl.DeviceIdType.MESH,
        )

    sent = []
    kept = []

    def send(src, dst, device, index, recv=None):
        one = copy(src, dst, device, index, index if recv is None else recv)
        one.start()
        sent.append(one)

    def keep(src, dst, index):
        one = pltpu.make_async_copy(src, dst, lsem.at[index])
        one.start()
        kept.append(one)

    def arrived(dst, index):
        copy(dst, dst, sibling, 0, index).wait_recv()

    def piece(block, member, which=None):
        rows = pl.ds(pl.multiple_of(32 * member, 32), 32)
        return kv.at[block, :, rows, :] if which is None else kv.at[block, which, rows, :]

    def w_rows(place, core):
        return pl.ds(pl.multiple_of(HD * (2 * place + core), HD), HD)

    def w_pair(place):
        return pl.ds(pl.multiple_of(2 * HD * place, 2 * HD), 2 * HD)

    def col(start, width):
        return pl.ds(pl.multiple_of(start, 128), width)

    partners = [z_next, z_prev, sibling]
    partners += [at(z, x, yy(step), core) for step in (1, 3) for core in range(2)]
    partners += [at(z, xx(step), y, core) for step in (1, 3) for core in range(2)]
    partners += [at(z, x, yy(2), c), at(z, xx(2), y, c)]
    barrier = pltpu.get_barrier_semaphore()
    for device in partners:
        pl.semaphore_signal(barrier, inc=1, device_id=device, device_id_type=pl.DeviceIdType.MESH)
    own = pl.ds(pl.multiple_of(32 * r, 32), 32)
    kv[0, 0, own, :] = k_ref[...]
    kv[0, 1, own, :] = v_ref[...]
    pl.semaphore_wait(barrier, len(partners))

    for which in range(2):
        send(piece(0, r, which), piece(0, r, which), y_pair, KV_Y0 + which)
        send(piece(0, r, which), piece(1, r, which), z_next, KV_Z1 + which)
    send(piece(0, r), piece(0, r), sibling, KV_CA)
    wx, wy = wb.at[0], wb.at[1]
    for k in range(NC):
        for half in range(2):
            src = w_ref.at[:, pl.ds(half * HALF + k * CW, CW)]
            dst = wx.at[w_rows(x, c), pl.ds(k * CW, CW)]
            send(src, dst, at(z, xx(1), y, half), W_UP + 2 * k + half, W_UP + 2 * k + c)
            send(src, dst, at(z, xx(3), y, half), W_DOWN + 2 * k + half, W_DOWN + 2 * k + c)
    mine, theirs = odd_z * (PATH // 2), (1 - odd_z) * (PATH // 2)
    quad = PATH // 4

    def send_wy(place, first):
        for half in range(2):
            src = w_ref.at[:, col(half * HALF + PATH + mine, PATH // 2)]
            dst = wy.at[w_rows(y, c), col(mine, PATH // 2)]
            send(src, dst, at(z, x, place, half), first + half, first + c)

    send_wy(outer, V_OUT)
    for path, place in ((0, x), (1, y)):
        rows = w_rows(place, c)
        send(w_ref.at[:, col((1 - c) * HALF + path * PATH, PATH)], wb.at[path, rows, :], sibling, W_SIB + path)
        keep(w_ref.at[:, col(c * HALF + path * PATH, PATH)], wb.at[path, rows, :], L_W + path)

    def forward_wx(k):
        for core in range(2):
            arrived(wx.at[w_rows(xx(3), core), pl.ds(k * CW, CW)], W_UP + 2 * k + core)
        for core in range(2):
            arrived(wx.at[w_rows(xx(1), core), pl.ds(k * CW, CW)], W_DOWN + 2 * k + core)
        below = wx.at[w_pair(xx(3)), pl.ds(k * CW, CW // 2)]
        above = wx.at[w_pair(xx(1)), pl.ds(k * CW + CW // 2, CW // 2)]
        send(below, below, at(z, xx(1), y, c), W_FUP + k)
        send(above, above, at(z, xx(3), y, c), W_FDOWN + k)

    def share_wy(place, group):
        first = wy.at[w_pair(place), col(mine, quad)]
        second = wy.at[w_pair(place), col(mine + quad, quad)]
        send(second, second, z_next, V_ZUP + group)
        send(first, first, z_prev, V_ZDOWN + group)

    def forward_wy_outer():
        for core in range(2):
            arrived(wy.at[w_rows(outer, core), col(mine, PATH // 2)], V_OUT + core)
        part_b = wy.at[w_pair(outer), col(mine + quad, quad)]
        send(part_b, part_b, y_pair, V_FIN)
        share_wy(outer, 0)

    def forward_wy_inner():
        for core in range(2):
            arrived(wy.at[w_rows(inner, core), col(mine, PATH // 2)], V_IN + core)
        part_a = wy.at[w_pair(inner), col(mine, quad)]
        send(part_a, part_a, at(z, x, outer, c), V_FOUT)
        share_wy(inner, 1)

    def forward_wy_far():
        arrived(wy.at[w_pair(yy(2)), col(mine + quad, quad)], V_FIN)
        arrived(wy.at[w_pair(yy(2)), col(mine, quad)], V_FOUT)
        share_wy(yy(2), 2)

    scaled = q_ref[...].astype(jnp.float32).T * SCALE
    coarse = scaled.astype(jnp.bfloat16)
    q2[:HD] = coarse
    q2[HD:] = (scaled - coarse.astype(jnp.float32)).astype(jnp.bfloat16)
    base = z * T
    local = lax.broadcasted_iota(jnp.int32, (8, T), 1)
    begin = jnp.zeros((8, T), jnp.int32)
    for d in range(DOCS):
        start = starts_ref[d]
        begin = jnp.where(local + base >= start, start, begin)
    lo_ref[...] = jnp.maximum(begin - base + WINDOW, local + 1)

    def scores(block, offset, k0, q0, n_sub, width, diagonal):
        keys = kn[block, pl.ds(k0, TK), :]
        keys = jnp.concatenate([keys, keys], axis=1)
        values = jnp.concatenate(
            [kv[block, 1, :, pl.ds(k0, TK)], jnp.ones((16, TK), jnp.bfloat16)], axis=0
        )
        tiles = []
        for u in range(n_sub):
            columns = pl.ds(q0 + u * width, width)
            tiles.append(jnp.dot(keys, q2[:, columns], preferred_element_type=jnp.float32))
        for u in range(n_sub):
            columns = pl.ds(q0 + u * width, width)
            place = lax.broadcasted_iota(jnp.int32, (TK, width), 0)
            allowed = place >= lo_ref[:1, columns] - (offset + k0)
            if diagonal:
                query = lax.broadcasted_iota(jnp.int32, (1, width), 1) + (q0 + u * width - k0)
                allowed &= place <= query
            tile = jnp.where(allowed, tiles[u], NEG)
            top = jnp.max(tile, axis=0, keepdims=True)
            if not diagonal:
                before = m_ref[:1, columns]
                top = jnp.maximum(before, top)
                keep_ = jnp.exp2(before - top)
            weights = jnp.exp2(tile - top).astype(jnp.bfloat16)
            added = jnp.dot(values, weights, preferred_element_type=jnp.float32)
            m_ref[:1, columns] = top
            acc[:, columns] = added if diagonal else acc[:, columns] * keep_ + added

    arrived(piece(0, r ^ 2, 0), KV_Y0)
    arrived(piece(0, r ^ 2, 1), KV_Y0 + 1)
    send(piece(0, r ^ 2), piece(0, r ^ 2), sibling, KV_CB)
    arrived(piece(1, r, 0), KV_Z1)
    arrived(piece(1, r, 1), KV_Z1 + 1)
    for which in range(2):
        send(piece(1, r, which), piece(1, r, which), y_pair, KV_Y1 + which)
        send(piece(1, r, 1 - which), piece(2, r, 1 - which), z_next, KV_Z2A + 1 - which)
    send(piece(1, r), piece(1, r), sibling, KV_CA + 1)
    arrived(piece(0, r ^ 1), KV_CA)
    arrived(piece(0, r ^ 3), KV_CB)
    kn[0] = kv[0, 0].T

    @pl.loop(0, T // TK)
    def _(i):
        q0 = pl.multiple_of(i * TK, TK)
        scores(0, WINDOW, q0, q0, TK // TQ, TQ, True)

        @pl.loop(0, i)
        def _(k):
            scores(0, WINDOW, pl.multiple_of(k * TK, TK), q0, TK // TQ, TQ, False)

    arrived(piece(1, r ^ 2, 0), KV_Y1)
    send(piece(1, r ^ 2, 0), piece(2, r ^ 2, 0), z_next, KV_Z2B)
    arrived(piece(2, r, 1), KV_Z2A + 1)
    send(piece(2, r, 1), piece(2, r, 1), y_pair, KV_Y2)
    arrived(piece(1, r ^ 2, 1), KV_Y1 + 1)
    send(piece(1, r ^ 2), piece(1, r ^ 2), sibling, KV_CB + 1)
    arrived(piece(2, r, 0), KV_Z2A)
    send(piece(2, r), piece(2, r), sibling, KV_CA + 2)
    send_wy(inner, V_IN)
    forward_wx(0)
    arrived(piece(1, r ^ 1), KV_CA + 1)
    arrived(piece(1, r ^ 3), KV_CB + 1)
    kn[1] = kv[1, 0].T

    for i in range(T // TK):

        @pl.loop(0, T // TK)
        def _(k):
            scores(1, T, pl.multiple_of(k * TK, TK), i * TK, TK // TQ, TQ, False)

        if i == 0:
            arrived(piece(2, r ^ 2, 0), KV_Z2B)
            send(piece(2, r ^ 2, 0), piece(2, r ^ 2, 0), sibling, KV_CB2)
            arrived(piece(2, r ^ 2, 1), KV_Y2)
            send(piece(2, r ^ 2, 1), piece(2, r ^ 2, 1), sibling, KV_CB2 + 1)
            forward_wx(1)
            forward_wy_outer()

    arrived(piece(2, r ^ 1), KV_CA + 2)
    arrived(piece(2, r ^ 3, 0), KV_CB2)
    arrived(piece(2, r ^ 3, 1), KV_CB2 + 1)
    kn[2] = kv[2, 0].T

    att_x, att_y = att.at[0], att.at[1]
    x_slot, y_slot = w_rows(x, c), w_rows(y, c)

    def sub_rows(place):
        return pl.ds(pl.multiple_of(place * SUB, SUB), SUB)

    for i, step in enumerate((2, 1, 3, 0)):
        quarter = xx(step)
        q0 = pl.multiple_of(quarter * QT, QT)

        @pl.loop(q0 // TK, T // TK)
        def _(k):
            scores(2, 0, pl.multiple_of(k * TK, TK), q0, 2, QT // 2, False)

        columns = pl.ds(q0, QT)
        total = acc[HD : HD + 1, columns]
        obuf[i] = (acc[:HD, columns] * (1.0 / total)).T.astype(jnp.bfloat16)
        if step:
            send(obuf.at[i], att_x.at[:, x_slot], at(z, quarter, y, c), A_X + step - 1)
        else:
            send(obuf.at[i], att_x.at[:, x_slot], sibling, A_XSIB)
            keep(obuf.at[i], att_x.at[:, x_slot], L_ATT)
        for away in (2, 1, 3):
            send(
                obuf.at[i, sub_rows(yy(away)), :],
                att_y.at[sub_rows(quarter), y_slot],
                at(z, x, yy(away), c),
                A_Y + 4 * (away - 1) + step,
            )
        keep(obuf.at[i, sub_rows(y), :], att_y.at[sub_rows(quarter), y_slot], L_ATT + 1 + i)
        if i == 1:
            forward_wy_inner()
    for one in kept[-5:]:
        one.wait()
    send(att_y.at[:, y_slot], att_y.at[:, y_slot], sibling, A_YSIB)
    for step in (2, 1, 3):
        slot = att_x.at[:, w_rows(xx(4 - step), c)]
        arrived(slot, A_X + step - 1)
        send(slot, slot, sibling, A_XSIB + step)
        slot = w_rows(yy(4 - step), c)
        for quarter in range(X):
            arrived(att_y.at[sub_rows(xx(quarter)), slot], A_Y + 4 * (step - 1) + quarter)
        send(att_y.at[:, slot], att_y.at[:, slot], sibling, A_YSIB + step)
    forward_wy_far()
    arrived(wx.at[w_rows(x, 1 - c), :], W_SIB)
    arrived(wy.at[w_rows(y, 1 - c), :], W_SIB + 1)
    for one in kept[:2]:
        one.wait()
    for step in range(4):
        arrived(att_x.at[:, w_rows(xx(4 - step), 1 - c)], A_XSIB + step)
    for step in range(4):
        arrived(att_y.at[:, w_rows(yy(4 - step), 1 - c)], A_YSIB + step)

    left, right = pl.ds(0, CW // 2), pl.ds(CW // 2, CW // 2)
    away = (yy, xx)

    def device(path, step):
        return at(z, x, yy(step), c) if path == 0 else at(z, xx(step), y, c)

    def chunk_of(path, k):
        return k * CW if path == 0 else (mine if k == 0 else theirs)

    def sub(j, block, half):
        return part[j, sub_rows(block), half]

    def project(path, k):
        j = 2 * k + path
        if path == 0:
            arrived(wx.at[w_pair(xx(2)), pl.ds(k * CW, CW // 2)], W_FUP + k)
            arrived(wx.at[w_pair(xx(2)), pl.ds(k * CW + CW // 2, CW // 2)], W_FDOWN + k)
        elif k == 1:
            for group, place in enumerate((outer, inner, yy(2))):
                arrived(wy.at[w_pair(place), col(theirs + quad, quad)], V_ZUP + group)
                arrived(wy.at[w_pair(place), col(theirs, quad)], V_ZDOWN + group)
        near, step = away[path], R_UP + 7 * j
        weight = wb[path, :, col(chunk_of(path, k), CW)]
        part[j] = jnp.dot(att[path], weight, preferred_element_type=jnp.float32)
        rel[j, 0] = sub(j, near(2), left).astype(jnp.bfloat16)
        send(rel.at[j, 0], rin.at[j, 0], device(path, 1), step)
        rel[j, 1] = sub(j, near(2), right).astype(jnp.bfloat16)
        send(rel.at[j, 1], rin.at[j, 1], device(path, 3), step + 1)
        msg[j, 0] = sub(j, near(1), right).astype(jnp.bfloat16)
        send(msg.at[j, 0], min_.at[j, 0], device(path, 1), step + 2)
        msg[j, 1] = sub(j, near(3), left).astype(jnp.bfloat16)
        send(msg.at[j, 1], min_.at[j, 1], device(path, 3), step + 3)

    def relay(path, k):
        j = 2 * k + path
        near, step = away[path], R_UP + 7 * j
        arrived(rin.at[j, 0], step)
        msg[j, 2] = (sub(j, near(1), left) + rin[j, 0].astype(jnp.float32)).astype(jnp.bfloat16)
        send(msg.at[j, 2], min_.at[j, 2], device(path, 1), step + 4)
        arrived(rin.at[j, 1], step + 1)
        msg[j, 3] = (sub(j, near(3), right) + rin[j, 1].astype(jnp.float32)).astype(jnp.bfloat16)
        send(msg.at[j, 3], min_.at[j, 3], device(path, 3), step + 5)

    def finish(path, k):
        j = 2 * k + path
        step = R_UP + 7 * j
        for one in range(4):
            arrived(min_.at[j, one], step + 2 + one)
        for columns, first, second in ((left, 1, 2), (right, 0, 3)):
            total = sub(j, x if path else y, columns) + min_[j, first].astype(jnp.float32)
            total += min_[j, second].astype(jnp.float32)
            res[j, :, columns] = total.astype(jnp.bfloat16)
        place = out_ref.at[:, col(c * HALF + path * PATH + chunk_of(path, k), CW)]
        rows = SUB // 2
        keep(res.at[j, pl.ds(pl.multiple_of(c * rows, rows), rows), :], place, L_OUT + j)
        other = pl.ds(pl.multiple_of((1 - c) * rows, rows), rows)
        send(res.at[j, other, :], place, sibling, step + 6)

    order = [(path, k) for k in range(NC) for path in range(2)]
    for n in range(len(order) + 4):
        if n < len(order):
            project(*order[n])
        if 2 <= n < len(order) + 2:
            relay(*order[n - 2])
        if n >= 4:
            finish(*order[n - 4])
    for path, k in order:
        place = out_ref.at[:, col((1 - c) * HALF + path * PATH + chunk_of(path, k), CW)]
        arrived(place, R_UP + 7 * (2 * k + path) + 6)
    for one in kept[-len(order) :]:
        one.wait()
    for one in sent:
        one.wait_send()


def on_device(queries, keys, values, out_weight, doc_starts):
    bf16, f32 = jnp.bfloat16, jnp.float32
    vmem = pl.BlockSpec(memory_space=pltpu.VMEM)
    return pl.pallas_call(
        kernel,
        out_shape=jax.ShapeDtypeStruct((SUB // 2, D), bf16),
        in_specs=[pl.BlockSpec(memory_space=pltpu.SMEM), vmem, vmem, vmem, vmem],
        out_specs=pl.BlockSpec(memory_space=pl.ANY),
        scratch_shapes=[
            pltpu.VMEM((3, 2, HD, T), bf16),
            pltpu.VMEM((3, T, HD), bf16),
            pltpu.VMEM((2 * HD, T), bf16),
            pltpu.VMEM((8, T), jnp.int32),
            pltpu.VMEM((8, T), f32),
            pltpu.VMEM((HD + 16, T), f32),
            pltpu.VMEM((X, QT, HD), bf16),
            pltpu.VMEM((2, QT, 2 * X * HD), bf16),
            pltpu.VMEM((2, 2 * X * HD, PATH), bf16),
            pltpu.VMEM((2 * NC, QT, CW), f32),
            pltpu.VMEM((2 * NC, 2, SUB, CW // 2), bf16),
            pltpu.VMEM((2 * NC, 2, SUB, CW // 2), bf16),
            pltpu.VMEM((2 * NC, 4, SUB, CW // 2), bf16),
            pltpu.VMEM((2 * NC, 4, SUB, CW // 2), bf16),
            pltpu.VMEM((2 * NC, SUB, CW), bf16),
            pltpu.SemaphoreType.DMA((N_COPIES,)),
            pltpu.SemaphoreType.DMA((N_COPIES,)),
            pltpu.SemaphoreType.DMA((N_LOCAL,)),
        ],
        compiler_params=pltpu.CompilerParams(
            collective_id=0, has_side_effects=True, vmem_limit_bytes=56 * 2**20
        ),
    )(doc_starts, queries, keys.T, values.T, out_weight)


def solution(mesh):
    placed = (P("ctx", "head"), P("ctx", "head"), P("ctx", "head"), P("head", None), P())
    return jax.shard_map(
        on_device, mesh=mesh, in_specs=placed, out_specs=P(("ctx", "head"), None), check_vma=False
    )
```

time: 75.7 us -> 69.6 us (0.919)
  Pallas kernels: 73.6 us -> 67.5 us
    pallas_call x1, Pallas kernels: 73.6 us -> 67.5 us  [on_device(): pl.pallas_call(kernel, out_shape=jax.ShapeDtypeStruct((SUB // 2, D), bf16...]
where the time goes in v2:
time: 69.6 us; the launch traced here: 69.4 us
  Pallas kernels  67.5 us (97%)
  local copies, waits for them, and re-layouts  1.87 us (3%)
    pallas_call x1, Pallas kernels, on_device(): pl.pallas_call(kernel, out_shape=jax.ShapeDtypeStruct((SUB // 2, D), bf16...  67.5 us
    unnamed x1, local copies, waits for them, and re-layouts  1.87 us

profile of v2, /device:TPU:1, one launch (start us, length us, event | category | flops | bytes accessed | tf_op | source)
XLA Modules:
  0.0 69.4 jit_solution(4586884615073268037)
XLA Ops:
  0.0 67.5 %shard_map.55 = bf16[64,4096]{1,0:T(8,128)(2,1)} custom-call(s32[16]{0:T(128)} %starts_ref.1, bf16[2048,128]{1,0:T(8,128)(2,1)} %q_ref.1, bf16[32,2048]{1,0:T(8,128)(2,1)} %bitcast.2, bf16[32,2048]{1,0:T(8,128)(2,1)} %bitcast.3, bf16[128,4096]{1,0:T(8,128)(2,1)} %w_ref.1), custom_call_target="tpu_custom_call" | custom-call | tf_op jit(solution)/shard_map/pallas_call | solution.py:404
  67.5 1.9 %copy.7 = bf16[64,4096]{1,0:T(8,128)(2,1)} copy(bf16[64,4096]{1,0:T(8,128)(2,1)} %shard_map.55) | data formatting | bytes 1048576

commit v3 on v2

--- a/solution.py
+++ b/solution.py
@@ -23,12 +23,14 @@
 NEG = -1e30
 SCALE = 1.4426950408889634 * HD**-0.5
 
+ORDER = (2, 1, 3, 0)
+
 KV_Y0, KV_Y1, KV_Y2, KV_Z1, KV_Z2A, KV_Z2B = 0, 2, 4, 5, 7, 9
-KV_CA, KV_CB, KV_CB2 = 10, 13, 15
-W_UP, W_DOWN, W_FUP, W_FDOWN, W_SIB = 17, 21, 25, 27, 29
-V_IN, V_OUT, V_FIN, V_FOUT, V_ZUP, V_ZDOWN = 31, 33, 35, 36, 37, 40
-A_X, A_Y, A_XSIB, A_YSIB = 43, 46, 58, 62
-R_UP = 66
+KV_CA0, KV_CB0, KV_CA1, KV_CB1, KV_CA2, KV_CB2 = 10, 12, 14, 15, 16, 17
+W_UP, W_DOWN, W_FUP, W_FDOWN, W_SIB = 19, 23, 27, 29, 31
+V_IN, V_OUT, V_FIN, V_FOUT, V_ZUP, V_ZDOWN, V_ZEDGE = 33, 35, 37, 38, 39, 42, 45
+A_X, A_Y, A_XSIB, A_YOWN, A_YF = 48, 51, 63, 67, 71
+R_UP = 77
 N_COPIES = R_UP + 7 * 2 * NC
 L_W, L_ATT, L_OUT = 0, 2, 7
 N_LOCAL = L_OUT + 2 * NC
@@ -58,6 +60,7 @@
 
     z_next = at(lax.rem(z + 1, Z), x, y, c)
     z_prev = at(lax.rem(z + Z - 1, Z), x, y, c)
+    has_next, has_one, has_two = z < Z - 1, z >= 1, z >= 2
     sibling = at(z, x, y, 1 - c)
     inner = yy(1 + 2 * odd_y)
     outer = yy(3 - 2 * odd_y)
@@ -73,25 +76,32 @@
             device_id_type=pl.DeviceIdType.MESH,
         )
 
+    def do(action, when):
+        if when is None:
+            action()
+        else:
+            pl.when(when)(action)
+
     sent = []
     kept = []
 
-    def send(src, dst, device, index, recv=None):
+    def send(src, dst, device, index, recv=None, when=None):
         one = copy(src, dst, device, index, index if recv is None else recv)
-        one.start()
-        sent.append(one)
+        do(one.start, when)
+        sent.append((one, when))
 
     def keep(src, dst, index):
         one = pltpu.make_async_copy(src, dst, lsem.at[index])
         one.start()
         kept.append(one)
 
-    def arrived(dst, index):
-        copy(dst, dst, sibling, 0, index).wait_recv()
-
-    def piece(block, member, which=None):
+    def arrived(dst, index, when=None):
+        do(copy(dst, dst, sibling, 0, index).wait_recv, when)
+
+    def piece(block, member, which=None, half=None):
         rows = pl.ds(pl.multiple_of(32 * member, 32), 32)
-        return kv.at[block, :, rows, :] if which is None else kv.at[block, which, rows, :]
+        tokens = pl.ds(0, T) if half is None else pl.ds(half * (T // 2), T // 2)
+        return kv.at[block, :, rows, tokens] if which is None else kv.at[block, which, rows, tokens]
 
     def w_rows(place, core):
         return pl.ds(pl.multiple_of(HD * (2 * place + core), HD), HD)
@@ -102,22 +112,29 @@
     def col(start, width):
         return pl.ds(pl.multiple_of(start, 128), width)
 
-    partners = [z_next, z_prev, sibling]
-    partners += [at(z, x, yy(step), core) for step in (1, 3) for core in range(2)]
-    partners += [at(z, xx(step), y, core) for step in (1, 3) for core in range(2)]
-    partners += [at(z, x, yy(2), c), at(z, xx(2), y, c)]
+    partners = [(sibling, None), (z_next, has_next), (z_prev, has_one)]
+    partners += [(at(z, x, yy(step), core), None) for step in (1, 3) for core in range(2)]
+    partners += [(at(z, xx(step), y, core), None) for step in (1, 3) for core in range(2)]
+    partners += [(at(z, x, yy(2), c), None), (at(z, xx(2), y, c), None)]
     barrier = pltpu.get_barrier_semaphore()
-    for device in partners:
-        pl.semaphore_signal(barrier, inc=1, device_id=device, device_id_type=pl.DeviceIdType.MESH)
+    for device, when in partners:
+
+        def greet(device=device):
+            pl.semaphore_signal(barrier, inc=1, device_id=device, device_id_type=pl.DeviceIdType.MESH)
+
+        do(greet, when)
     own = pl.ds(pl.multiple_of(32 * r, 32), 32)
     kv[0, 0, own, :] = k_ref[...]
     kv[0, 1, own, :] = v_ref[...]
-    pl.semaphore_wait(barrier, len(partners))
-
-    for which in range(2):
-        send(piece(0, r, which), piece(0, r, which), y_pair, KV_Y0 + which)
-        send(piece(0, r, which), piece(1, r, which), z_next, KV_Z1 + which)
-    send(piece(0, r), piece(0, r), sibling, KV_CA)
+    at_edge = jnp.where(has_next, 0, 1) + jnp.where(has_one, 0, 1)
+    pl.semaphore_wait(barrier, len(partners) - at_edge)
+
+    send(piece(0, r, half=0), piece(0, r, half=0), y_pair, KV_Y0)
+    send(piece(0, r, 0), piece(1, r, 0), z_next, KV_Z1, when=has_next)
+    send(piece(0, r, half=0), piece(0, r, half=0), sibling, KV_CA0)
+    send(piece(0, r, half=1), piece(0, r, half=1), y_pair, KV_Y0 + 1)
+    send(piece(0, r, 1), piece(1, r, 1), z_next, KV_Z1 + 1, when=has_next)
+    send(piece(0, r, half=1), piece(0, r, half=1), sibling, KV_CA0 + 1)
     wx, wy = wb.at[0], wb.at[1]
     for k in range(NC):
         for half in range(2):
@@ -153,8 +170,12 @@
     def share_wy(place, group):
         first = wy.at[w_pair(place), col(mine, quad)]
         second = wy.at[w_pair(place), col(mine + quad, quad)]
-        send(second, second, z_next, V_ZUP + group)
-        send(first, first, z_prev, V_ZDOWN + group)
+        send(second, second, z_next, V_ZUP + group, when=has_next)
+        send(first, first, z_prev, V_ZDOWN + group, when=has_one)
+        send(second, second, z_prev, V_ZEDGE + group, V_ZUP + group, when=z == 1)
+        up = copy(first, first, z_next, V_ZEDGE + group, V_ZDOWN + group)
+        do(up.start, z == Z - 2)
+        sent.append((up, z == Z - 2))
 
     def forward_wy_outer():
         for core in range(2):
@@ -187,19 +208,22 @@
         begin = jnp.where(local + base >= start, start, begin)
     lo_ref[...] = jnp.maximum(begin - base + WINDOW, local + 1)
 
-    def scores(block, offset, k0, q0, n_sub, width, diagonal):
-        keys = kn[block, pl.ds(k0, TK), :]
+    def scores(block, offset, k0, q0, width, span=TK, diagonal=False):
+        keys = kn[block, pl.ds(k0, span), :]
         keys = jnp.concatenate([keys, keys], axis=1)
         values = jnp.concatenate(
-            [kv[block, 1, :, pl.ds(k0, TK)], jnp.ones((16, TK), jnp.bfloat16)], axis=0
+            [kv[block, 1, :, pl.ds(k0, span)], jnp.ones((16, span), jnp.bfloat16)], axis=0
         )
         tiles = []
-        for u in range(n_sub):
+        spans = [(u + 1) * width if diagonal else span for u in range(2)]
+        for u in range(2):
             columns = pl.ds(q0 + u * width, width)
-            tiles.append(jnp.dot(keys, q2[:, columns], preferred_element_type=jnp.float32))
-        for u in range(n_sub):
+            tiles.append(
+                jnp.dot(keys[: spans[u]], q2[:, columns], preferred_element_type=jnp.float32)
+            )
+        for u in range(2):
             columns = pl.ds(q0 + u * width, width)
-            place = lax.broadcasted_iota(jnp.int32, (TK, width), 0)
+            place = lax.broadcasted_iota(jnp.int32, (spans[u], width), 0)
             allowed = place >= lo_ref[:1, columns] - (offset + k0)
             if diagonal:
                 query = lax.broadcasted_iota(jnp.int32, (1, width), 1) + (q0 + u * width - k0)
@@ -211,64 +235,70 @@
                 top = jnp.maximum(before, top)
                 keep_ = jnp.exp2(before - top)
             weights = jnp.exp2(tile - top).astype(jnp.bfloat16)
-            added = jnp.dot(values, weights, preferred_element_type=jnp.float32)
+            added = jnp.dot(values[:, : spans[u]], weights, preferred_element_type=jnp.float32)
             m_ref[:1, columns] = top
             acc[:, columns] = added if diagonal else acc[:, columns] * keep_ + added
 
-    arrived(piece(0, r ^ 2, 0), KV_Y0)
-    arrived(piece(0, r ^ 2, 1), KV_Y0 + 1)
-    send(piece(0, r ^ 2), piece(0, r ^ 2), sibling, KV_CB)
-    arrived(piece(1, r, 0), KV_Z1)
-    arrived(piece(1, r, 1), KV_Z1 + 1)
-    for which in range(2):
-        send(piece(1, r, which), piece(1, r, which), y_pair, KV_Y1 + which)
-        send(piece(1, r, 1 - which), piece(2, r, 1 - which), z_next, KV_Z2A + 1 - which)
-    send(piece(1, r), piece(1, r), sibling, KV_CA + 1)
-    arrived(piece(0, r ^ 1), KV_CA)
-    arrived(piece(0, r ^ 3), KV_CB)
-    kn[0] = kv[0, 0].T
-
-    @pl.loop(0, T // TK)
-    def _(i):
-        q0 = pl.multiple_of(i * TK, TK)
-        scores(0, WINDOW, q0, q0, TK // TQ, TQ, True)
-
-        @pl.loop(0, i)
-        def _(k):
-            scores(0, WINDOW, pl.multiple_of(k * TK, TK), q0, TK // TQ, TQ, False)
-
-    arrived(piece(1, r ^ 2, 0), KV_Y1)
-    send(piece(1, r ^ 2, 0), piece(2, r ^ 2, 0), z_next, KV_Z2B)
-    arrived(piece(2, r, 1), KV_Z2A + 1)
-    send(piece(2, r, 1), piece(2, r, 1), y_pair, KV_Y2)
-    arrived(piece(1, r ^ 2, 1), KV_Y1 + 1)
-    send(piece(1, r ^ 2), piece(1, r ^ 2), sibling, KV_CB + 1)
-    arrived(piece(2, r, 0), KV_Z2A)
-    send(piece(2, r), piece(2, r), sibling, KV_CA + 2)
+    half_t = T // 2
+    arrived(piece(0, r ^ 2, half=0), KV_Y0)
+    send(piece(0, r ^ 2, half=0), piece(0, r ^ 2, half=0), sibling, KV_CB0)
+    arrived(piece(1, r, 0), KV_Z1, when=has_one)
+    send(piece(1, r, 0), piece(1, r, 0), y_pair, KV_Y1, when=has_one)
+    send(piece(1, r, 0), piece(2, r, 0), z_next, KV_Z2A, when=has_one & has_next)
+    arrived(piece(0, r ^ 1, half=0), KV_CA0)
+    arrived(piece(0, r ^ 3, half=0), KV_CB0)
+    kn[0, pl.ds(0, half_t)] = kv[0, 0, :, pl.ds(0, half_t)].T
+    scores(0, WINDOW, 0, 0, TQ, diagonal=True)
+    arrived(piece(0, r ^ 2, half=1), KV_Y0 + 1)
+    send(piece(0, r ^ 2, half=1), piece(0, r ^ 2, half=1), sibling, KV_CB0 + 1)
+    arrived(piece(1, r, 1), KV_Z1 + 1, when=has_one)
+    send(piece(1, r, 1), piece(1, r, 1), y_pair, KV_Y1 + 1, when=has_one)
+    send(piece(1, r, 1), piece(2, r, 1), z_next, KV_Z2A + 1, when=has_one & has_next)
+    send(piece(1, r), piece(1, r), sibling, KV_CA1, when=has_one)
+    arrived(piece(0, r ^ 1, half=1), KV_CA0 + 1)
+    arrived(piece(0, r ^ 3, half=1), KV_CB0 + 1)
+    kn[0, pl.ds(half_t, half_t)] = kv[0, 0, :, pl.ds(half_t, half_t)].T
+    scores(0, WINDOW, half_t, half_t, TQ, diagonal=True)
+    arrived(piece(1, r ^ 2, 0), KV_Y1, when=has_one)
+    send(piece(1, r ^ 2, 0), piece(2, r ^ 2, 0), z_next, KV_Z2B, when=has_one & has_next)
+    scores(0, WINDOW, 0, half_t, TQ)
+
+    arrived(piece(2, r, 1), KV_Z2A + 1, when=has_two)
+    send(piece(2, r, 1), piece(2, r, 1), y_pair, KV_Y2, when=has_two)
+    arrived(piece(1, r ^ 2, 1), KV_Y1 + 1, when=has_one)
+    send(piece(1, r ^ 2), piece(1, r ^ 2), sibling, KV_CB1, when=has_one)
+    arrived(piece(2, r, 0), KV_Z2A, when=has_two)
+    send(piece(2, r), piece(2, r), sibling, KV_CA2, when=has_two)
     send_wy(inner, V_IN)
     forward_wx(0)
-    arrived(piece(1, r ^ 1), KV_CA + 1)
-    arrived(piece(1, r ^ 3), KV_CB + 1)
-    kn[1] = kv[1, 0].T
+    arrived(piece(1, r ^ 1), KV_CA1, when=has_one)
+    arrived(piece(1, r ^ 3), KV_CB1, when=has_one)
 
     for i in range(T // TK):
 
-        @pl.loop(0, T // TK)
-        def _(k):
-            scores(1, T, pl.multiple_of(k * TK, TK), i * TK, TK // TQ, TQ, False)
+        @pl.when(has_one)
+        def _():
+            if i == 0:
+                kn[1] = kv[1, 0].T
+
+            @pl.loop(0, T // TK)
+            def _(k):
+                scores(1, T, pl.multiple_of(k * TK, TK), i * TK, TQ)
 
         if i == 0:
-            arrived(piece(2, r ^ 2, 0), KV_Z2B)
-            send(piece(2, r ^ 2, 0), piece(2, r ^ 2, 0), sibling, KV_CB2)
-            arrived(piece(2, r ^ 2, 1), KV_Y2)
-            send(piece(2, r ^ 2, 1), piece(2, r ^ 2, 1), sibling, KV_CB2 + 1)
+            for which, index in ((0, KV_Z2B), (1, KV_Y2)):
+                arrived(piece(2, r ^ 2, which), index, when=has_two)
+                send(piece(2, r ^ 2, which), piece(2, r ^ 2, which), sibling, KV_CB2 + which, when=has_two)
             forward_wx(1)
             forward_wy_outer()
 
-    arrived(piece(2, r ^ 1), KV_CA + 2)
-    arrived(piece(2, r ^ 3, 0), KV_CB2)
-    arrived(piece(2, r ^ 3, 1), KV_CB2 + 1)
-    kn[2] = kv[2, 0].T
+    arrived(piece(2, r ^ 1), KV_CA2, when=has_two)
+    arrived(piece(2, r ^ 3, 0), KV_CB2, when=has_two)
+    arrived(piece(2, r ^ 3, 1), KV_CB2 + 1, when=has_two)
+
+    @pl.when(has_two)
+    def _():
+        kn[2] = kv[2, 0].T
 
     att_x, att_y = att.at[0], att.at[1]
     x_slot, y_slot = w_rows(x, c), w_rows(y, c)
@@ -276,13 +306,31 @@
     def sub_rows(place):
         return pl.ds(pl.multiple_of(place * SUB, SUB), SUB)
 
-    for i, step in enumerate((2, 1, 3, 0)):
+    def forward_x(step):
+        slot = att_x.at[:, w_rows(xx(4 - step), c)]
+        arrived(slot, A_X + step - 1)
+        send(slot, slot, sibling, A_XSIB + step)
+
+    def forward_y(step, half):
+        slot = w_rows(yy(4 - step), c)
+        for i in (2 * half, 2 * half + 1):
+            arrived(att_y.at[sub_rows(i), slot], A_Y + 4 * (step - 1) + i)
+        both = att_y.at[pl.ds(2 * SUB * half, 2 * SUB), slot]
+        send(both, both, sibling, A_YF + 2 * (step - 1) + half)
+
+    for i, step in enumerate(ORDER):
         quarter = xx(step)
         q0 = pl.multiple_of(quarter * QT, QT)
 
-        @pl.loop(q0 // TK, T // TK)
-        def _(k):
-            scores(2, 0, pl.multiple_of(k * TK, TK), q0, 2, QT // 2, False)
+        @pl.when(has_two & (lax.rem(quarter, 2) == 1))
+        def _():
+            scores(2, 0, q0, q0, QT // 2, span=QT)
+
+        @pl.when(has_two)
+        def _():
+            @pl.loop((quarter + 1) // 2, T // TK)
+            def _(k):
+                scores(2, 0, pl.multiple_of(k * TK, TK), q0, QT // 2)
 
         columns = pl.ds(q0, QT)
         total = acc[HD : HD + 1, columns]
@@ -295,37 +343,32 @@
         for away in (2, 1, 3):
             send(
                 obuf.at[i, sub_rows(yy(away)), :],
-                att_y.at[sub_rows(quarter), y_slot],
+                att_y.at[sub_rows(i), y_slot],
                 at(z, x, yy(away), c),
-                A_Y + 4 * (away - 1) + step,
+                A_Y + 4 * (away - 1) + i,
             )
-        keep(obuf.at[i, sub_rows(y), :], att_y.at[sub_rows(quarter), y_slot], L_ATT + 1 + i)
+        send(obuf.at[i, sub_rows(y), :], att_y.at[sub_rows(i), y_slot], sibling, A_YOWN + i)
+        keep(obuf.at[i, sub_rows(y), :], att_y.at[sub_rows(i), y_slot], L_ATT + 1 + i)
         if i == 1:
             forward_wy_inner()
-    for one in kept[-5:]:
-        one.wait()
-    send(att_y.at[:, y_slot], att_y.at[:, y_slot], sibling, A_YSIB)
-    for step in (2, 1, 3):
-        slot = att_x.at[:, w_rows(xx(4 - step), c)]
-        arrived(slot, A_X + step - 1)
-        send(slot, slot, sibling, A_XSIB + step)
-        slot = w_rows(yy(4 - step), c)
-        for quarter in range(X):
-            arrived(att_y.at[sub_rows(xx(quarter)), slot], A_Y + 4 * (step - 1) + quarter)
-        send(att_y.at[:, slot], att_y.at[:, slot], sibling, A_YSIB + step)
+        if i == 2:
+            forward_x(2)
+            for away in (2, 1, 3):
+                forward_y(away, 0)
+    for away in (1, 3):
+        forward_x(away)
+    for away in (2, 1, 3):
+        forward_y(away, 1)
     forward_wy_far()
     arrived(wx.at[w_rows(x, 1 - c), :], W_SIB)
     arrived(wy.at[w_rows(y, 1 - c), :], W_SIB + 1)
-    for one in kept[:2]:
+    for one in kept:
         one.wait()
+    del kept[:]
     for step in range(4):
         arrived(att_x.at[:, w_rows(xx(4 - step), 1 - c)], A_XSIB + step)
-    for step in range(4):
-        arrived(att_y.at[:, w_rows(yy(4 - step), 1 - c)], A_YSIB + step)
 
     left, right = pl.ds(0, CW // 2), pl.ds(CW // 2, CW // 2)
-    away = (yy, xx)
-
     def device(path, step):
         return at(z, x, yy(step), c) if path == 0 else at(z, xx(step), y, c)
 
@@ -334,6 +377,9 @@
 
     def sub(j, block, half):
         return part[j, sub_rows(block), half]
+
+    def block_of(path, step):
+        return yy(step) if path == 0 else ORDER.index(step)
 
     def project(path, k):
         j = 2 * k + path
@@ -344,26 +390,33 @@
             for group, place in enumerate((outer, inner, yy(2))):
                 arrived(wy.at[w_pair(place), col(theirs + quad, quad)], V_ZUP + group)
                 arrived(wy.at[w_pair(place), col(theirs, quad)], V_ZDOWN + group)
-        near, step = away[path], R_UP + 7 * j
+        step = R_UP + 7 * j
+        if path == 1 and k == 0:
+            for i in range(4):
+                arrived(att_y.at[sub_rows(i), w_rows(y, 1 - c)], A_YOWN + i)
+            for away in (1, 2, 3):
+                for half in range(2):
+                    both = att_y.at[pl.ds(2 * SUB * half, 2 * SUB), w_rows(yy(4 - away), 1 - c)]
+                    arrived(both, A_YF + 2 * (away - 1) + half)
         weight = wb[path, :, col(chunk_of(path, k), CW)]
         part[j] = jnp.dot(att[path], weight, preferred_element_type=jnp.float32)
-        rel[j, 0] = sub(j, near(2), left).astype(jnp.bfloat16)
+        rel[j, 0] = sub(j, block_of(path, 2), left).astype(jnp.bfloat16)
         send(rel.at[j, 0], rin.at[j, 0], device(path, 1), step)
-        rel[j, 1] = sub(j, near(2), right).astype(jnp.bfloat16)
+        rel[j, 1] = sub(j, block_of(path, 2), right).astype(jnp.bfloat16)
         send(rel.at[j, 1], rin.at[j, 1], device(path, 3), step + 1)
-        msg[j, 0] = sub(j, near(1), right).astype(jnp.bfloat16)
+        msg[j, 0] = sub(j, block_of(path, 1), right).astype(jnp.bfloat16)
         send(msg.at[j, 0], min_.at[j, 0], device(path, 1), step + 2)
-        msg[j, 1] = sub(j, near(3), left).astype(jnp.bfloat16)
+        msg[j, 1] = sub(j, block_of(path, 3), left).astype(jnp.bfloat16)
         send(msg.at[j, 1], min_.at[j, 1], device(path, 3), step + 3)
 
     def relay(path, k):
         j = 2 * k + path
-        near, step = away[path], R_UP + 7 * j
+        step = R_UP + 7 * j
         arrived(rin.at[j, 0], step)
-        msg[j, 2] = (sub(j, near(1), left) + rin[j, 0].astype(jnp.float32)).astype(jnp.bfloat16)
+        msg[j, 2] = (sub(j, block_of(path, 1), left) + rin[j, 0].astype(jnp.float32)).astype(jnp.bfloat16)
         send(msg.at[j, 2], min_.at[j, 2], device(path, 1), step + 4)
         arrived(rin.at[j, 1], step + 1)
-        msg[j, 3] = (sub(j, near(3), right) + rin[j, 1].astype(jnp.float32)).astype(jnp.bfloat16)
+        msg[j, 3] = (sub(j, block_of(path, 3), right) + rin[j, 1].astype(jnp.float32)).astype(jnp.bfloat16)
         send(msg.at[j, 3], min_.at[j, 3], device(path, 3), step + 5)
 
     def finish(path, k):
@@ -372,7 +425,7 @@
         for one in range(4):
             arrived(min_.at[j, one], step + 2 + one)
         for columns, first, second in ((left, 1, 2), (right, 0, 3)):
-            total = sub(j, x if path else y, columns) + min_[j, first].astype(jnp.float32)
+            total = sub(j, block_of(path, 0), columns) + min_[j, first].astype(jnp.float32)
             total += min_[j, second].astype(jnp.float32)
             res[j, :, columns] = total.astype(jnp.bfloat16)
         place = out_ref.at[:, col(c * HALF + path * PATH + chunk_of(path, k), CW)]
@@ -392,10 +445,10 @@
     for path, k in order:
         place = out_ref.at[:, col((1 - c) * HALF + path * PATH + chunk_of(path, k), CW)]
         arrived(place, R_UP + 7 * (2 * k + path) + 6)
-    for one in kept[-len(order) :]:
+    for one in kept:
         one.wait()
-    for one in sent:
-        one.wait_send()
+    for one, when in sent:
+        do(one.wait_send, when)
 
 
 def on_device(queries, keys, values, out_weight, doc_starts):

time: 69.6 us -> 62.4 us (0.90)
  the two profiles are of different devices: /device:TPU:1 before, /device:TPU:97 now
where the time goes in v3:
time: 62.4 us; the launch traced here: 62.2 us
  Pallas kernels  60.3 us (97%)
  local copies, waits for them, and re-layouts  1.87 us (3%)
    pallas_call x1, Pallas kernels, on_device(): pl.pallas_call(kernel, out_shape=jax.ShapeDtypeStruct((SUB // 2, D), bf16...  60.3 us
    unnamed x1, local copies, waits for them, and re-layouts  1.87 us

profile of v3, /device:TPU:97, one launch (start us, length us, event | category | flops | bytes accessed | tf_op | source)
XLA Modules:
  0.0 62.2 jit_solution(753243988054416932)
XLA Ops:
  0.0 60.3 %shard_map.55 = bf16[64,4096]{1,0:T(8,128)(2,1)} custom-call(s32[16]{0:T(128)} %starts_ref.1, bf16[2048,128]{1,0:T(8,128)(2,1)} %q_ref.1, bf16[32,2048]{1,0:T(8,128)(2,1)} %bitcast.2, bf16[32,2048]{1,0:T(8,128)(2,1)} %bitcast.3, bf16[128,4096]{1,0:T(8,128)(2,1)} %w_ref.1), custom_call_target="tpu_custom_call" | custom-call | tf_op jit(solution)/shard_map/pallas_call | solution.py:457
  60.3 1.9 %copy.7 = bf16[64,4096]{1,0:T(8,128)(2,1)} copy(bf16[64,4096]{1,0:T(8,128)(2,1)} %shard_map.55) | data formatting | bytes 1048576

commit v4 on v3

--- a/solution.py
+++ b/solution.py
@@ -14,8 +14,9 @@
 Z, X, Y = 8, 4, 4
 HALF = D // 2
 PATH = HALF // 2
-CW = 512
+CW = 256
 NC = PATH // CW
+WC = 512
 QT = T // X
 SUB = QT // Y
 TQ = 512
@@ -25,12 +26,12 @@
 
 ORDER = (2, 1, 3, 0)
 
-KV_Y0, KV_Y1, KV_Y2, KV_Z1, KV_Z2A, KV_Z2B = 0, 2, 4, 5, 7, 9
-KV_CA0, KV_CB0, KV_CA1, KV_CB1, KV_CA2, KV_CB2 = 10, 12, 14, 15, 16, 17
-W_UP, W_DOWN, W_FUP, W_FDOWN, W_SIB = 19, 23, 27, 29, 31
-V_IN, V_OUT, V_FIN, V_FOUT, V_ZUP, V_ZDOWN, V_ZEDGE = 33, 35, 37, 38, 39, 42, 45
-A_X, A_Y, A_XSIB, A_YOWN, A_YF = 48, 51, 63, 67, 71
-R_UP = 77
+KV_Y0, KV_Y1, KV_Z1, KV_Z2, KV_FAR = 0, 2, 4, 6, 8
+KV_CA, KV_CB = 10, 16
+W_UP, W_DOWN, W_FUP, W_FDOWN, W_SIB = 22, 26, 30, 32, 34
+V_IN, V_OUT, V_FIN, V_FOUT, V_ZUP, V_ZDOWN, V_ZEDGE = 36, 38, 40, 41, 42, 45, 48
+A_X, A_Y, A_XSIB, A_YOWN, A_YF = 51, 54, 66, 70, 74
+R_UP = 80
 N_COPIES = R_UP + 7 * 2 * NC
 L_W, L_ATT, L_OUT = 0, 2, 7
 N_LOCAL = L_OUT + 2 * NC
@@ -98,10 +99,10 @@
     def arrived(dst, index, when=None):
         do(copy(dst, dst, sibling, 0, index).wait_recv, when)
 
-    def piece(block, member, which=None, half=None):
+    def piece(block, member, half):
         rows = pl.ds(pl.multiple_of(32 * member, 32), 32)
-        tokens = pl.ds(0, T) if half is None else pl.ds(half * (T // 2), T // 2)
-        return kv.at[block, :, rows, tokens] if which is None else kv.at[block, which, rows, tokens]
+        tokens = pl.ds(half * (T // 2), T // 2)
+        return kv.at[block, :, rows, tokens]
 
     def w_rows(place, core):
         return pl.ds(pl.multiple_of(HD * (2 * place + core), HD), HD)
@@ -129,17 +130,15 @@
     at_edge = jnp.where(has_next, 0, 1) + jnp.where(has_one, 0, 1)
     pl.semaphore_wait(barrier, len(partners) - at_edge)
 
-    send(piece(0, r, half=0), piece(0, r, half=0), y_pair, KV_Y0)
-    send(piece(0, r, 0), piece(1, r, 0), z_next, KV_Z1, when=has_next)
-    send(piece(0, r, half=0), piece(0, r, half=0), sibling, KV_CA0)
-    send(piece(0, r, half=1), piece(0, r, half=1), y_pair, KV_Y0 + 1)
-    send(piece(0, r, 1), piece(1, r, 1), z_next, KV_Z1 + 1, when=has_next)
-    send(piece(0, r, half=1), piece(0, r, half=1), sibling, KV_CA0 + 1)
+    for h in range(2):
+        send(piece(0, r, h), piece(0, r, h), y_pair, KV_Y0 + h)
+        send(piece(0, r, h), piece(1, r, h), z_next, KV_Z1 + h, when=has_next)
+        send(piece(0, r, h), piece(0, r, h), sibling, KV_CA + h)
     wx, wy = wb.at[0], wb.at[1]
-    for k in range(NC):
+    for k in range(2):
         for half in range(2):
-            src = w_ref.at[:, pl.ds(half * HALF + k * CW, CW)]
-            dst = wx.at[w_rows(x, c), pl.ds(k * CW, CW)]
+            src = w_ref.at[:, pl.ds(half * HALF + k * WC, WC)]
+            dst = wx.at[w_rows(x, c), pl.ds(k * WC, WC)]
             send(src, dst, at(z, xx(1), y, half), W_UP + 2 * k + half, W_UP + 2 * k + c)
             send(src, dst, at(z, xx(3), y, half), W_DOWN + 2 * k + half, W_DOWN + 2 * k + c)
     mine, theirs = odd_z * (PATH // 2), (1 - odd_z) * (PATH // 2)
@@ -159,11 +158,11 @@
 
     def forward_wx(k):
         for core in range(2):
-            arrived(wx.at[w_rows(xx(3), core), pl.ds(k * CW, CW)], W_UP + 2 * k + core)
+            arrived(wx.at[w_rows(xx(3), core), pl.ds(k * WC, WC)], W_UP + 2 * k + core)
         for core in range(2):
-            arrived(wx.at[w_rows(xx(1), core), pl.ds(k * CW, CW)], W_DOWN + 2 * k + core)
-        below = wx.at[w_pair(xx(3)), pl.ds(k * CW, CW // 2)]
-        above = wx.at[w_pair(xx(1)), pl.ds(k * CW + CW // 2, CW // 2)]
+            arrived(wx.at[w_rows(xx(1), core), pl.ds(k * WC, WC)], W_DOWN + 2 * k + core)
+        below = wx.at[w_pair(xx(3)), pl.ds(k * WC, WC // 2)]
+        above = wx.at[w_pair(xx(1)), pl.ds(k * WC + WC // 2, WC // 2)]
         send(below, below, at(z, xx(1), y, c), W_FUP + k)
         send(above, above, at(z, xx(3), y, c), W_FDOWN + k)
 
@@ -173,9 +172,7 @@
         send(second, second, z_next, V_ZUP + group, when=has_next)
         send(first, first, z_prev, V_ZDOWN + group, when=has_one)
         send(second, second, z_prev, V_ZEDGE + group, V_ZUP + group, when=z == 1)
-        up = copy(first, first, z_next, V_ZEDGE + group, V_ZDOWN + group)
-        do(up.start, z == Z - 2)
-        sent.append((up, z == Z - 2))
+        send(first, first, z_next, V_ZEDGE + group, V_ZDOWN + group, when=z == Z - 2)
 
     def forward_wy_outer():
         for core in range(2):
@@ -239,66 +236,85 @@
             m_ref[:1, columns] = top
             acc[:, columns] = added if diagonal else acc[:, columns] * keep_ + added
 
+    def turn(block, h):
+        half = pl.ds(h * (T // 2), T // 2)
+        kn[block, half] = kv[block, 0, :, half].T
+
+    def own_to_sibling(block, h, when):
+        send(piece(block, r, h), piece(block, r, h), sibling, KV_CA + 2 * block + h, when=when)
+
+    def pair_to_sibling(block, h, when=None):
+        member = r ^ 2
+        send(piece(block, member, h), piece(block, member, h), sibling, KV_CB + 2 * block + h, when=when)
+
+    def whole(block, h, when=None):
+        arrived(piece(block, r ^ 1, h), KV_CA + 2 * block + h, when=when)
+        arrived(piece(block, r ^ 3, h), KV_CB + 2 * block + h, when=when)
+
     half_t = T // 2
-    arrived(piece(0, r ^ 2, half=0), KV_Y0)
-    send(piece(0, r ^ 2, half=0), piece(0, r ^ 2, half=0), sibling, KV_CB0)
-    arrived(piece(1, r, 0), KV_Z1, when=has_one)
-    send(piece(1, r, 0), piece(1, r, 0), y_pair, KV_Y1, when=has_one)
-    send(piece(1, r, 0), piece(2, r, 0), z_next, KV_Z2A, when=has_one & has_next)
-    arrived(piece(0, r ^ 1, half=0), KV_CA0)
-    arrived(piece(0, r ^ 3, half=0), KV_CB0)
-    kn[0, pl.ds(0, half_t)] = kv[0, 0, :, pl.ds(0, half_t)].T
-    scores(0, WINDOW, 0, 0, TQ, diagonal=True)
-    arrived(piece(0, r ^ 2, half=1), KV_Y0 + 1)
-    send(piece(0, r ^ 2, half=1), piece(0, r ^ 2, half=1), sibling, KV_CB0 + 1)
-    arrived(piece(1, r, 1), KV_Z1 + 1, when=has_one)
-    send(piece(1, r, 1), piece(1, r, 1), y_pair, KV_Y1 + 1, when=has_one)
-    send(piece(1, r, 1), piece(2, r, 1), z_next, KV_Z2A + 1, when=has_one & has_next)
-    send(piece(1, r), piece(1, r), sibling, KV_CA1, when=has_one)
-    arrived(piece(0, r ^ 1, half=1), KV_CA0 + 1)
-    arrived(piece(0, r ^ 3, half=1), KV_CB0 + 1)
-    kn[0, pl.ds(half_t, half_t)] = kv[0, 0, :, pl.ds(half_t, half_t)].T
-    scores(0, WINDOW, half_t, half_t, TQ, diagonal=True)
+    for h in range(2):
+        arrived(piece(0, r ^ 2, h), KV_Y0 + h)
+        pair_to_sibling(0, h)
+        arrived(piece(1, r, h), KV_Z1 + h, when=has_one)
+        send(piece(1, r, h), piece(1, r, h), y_pair, KV_Y1 + h, when=has_one)
+        send(piece(1, r, h), piece(2, r, h), z_next, KV_Z2 + h, when=has_one & has_next)
+        own_to_sibling(1, h, has_one)
+        whole(0, h)
+        turn(0, h)
+        scores(0, WINDOW, h * half_t, h * half_t, TQ, diagonal=True)
     arrived(piece(1, r ^ 2, 0), KV_Y1, when=has_one)
-    send(piece(1, r ^ 2, 0), piece(2, r ^ 2, 0), z_next, KV_Z2B, when=has_one & has_next)
+    send(piece(1, r ^ 2, 0), piece(2, r ^ 2, 0), z_next, KV_FAR, when=has_one & has_next)
+    pair_to_sibling(1, 0, has_one)
+    arrived(piece(2, r, 0), KV_Z2, when=has_two)
+    own_to_sibling(2, 0, has_two)
     scores(0, WINDOW, 0, half_t, TQ)
 
-    arrived(piece(2, r, 1), KV_Z2A + 1, when=has_two)
-    send(piece(2, r, 1), piece(2, r, 1), y_pair, KV_Y2, when=has_two)
+    whole(1, 0, has_one)
+
+    def before(h, group):
+        scores(1, T, h * half_t, group * half_t, TQ)
+
+    @pl.when(has_one)
+    def _():
+        turn(1, 0)
+        before(0, 0)
+
     arrived(piece(1, r ^ 2, 1), KV_Y1 + 1, when=has_one)
-    send(piece(1, r ^ 2), piece(1, r ^ 2), sibling, KV_CB1, when=has_one)
-    arrived(piece(2, r, 0), KV_Z2A, when=has_two)
-    send(piece(2, r), piece(2, r), sibling, KV_CA2, when=has_two)
+    pair_to_sibling(1, 1, has_one)
+    arrived(piece(2, r, 1), KV_Z2 + 1, when=has_two)
+    send(piece(2, r, 1), piece(2, r, 1), y_pair, KV_FAR + 1, when=has_two)
+    own_to_sibling(2, 1, has_two)
     send_wy(inner, V_IN)
+
+    @pl.when(has_one)
+    def _():
+        before(0, 1)
+
     forward_wx(0)
-    arrived(piece(1, r ^ 1), KV_CA1, when=has_one)
-    arrived(piece(1, r ^ 3), KV_CB1, when=has_one)
-
-    for i in range(T // TK):
-
-        @pl.when(has_one)
-        def _():
-            if i == 0:
-                kn[1] = kv[1, 0].T
-
-            @pl.loop(0, T // TK)
-            def _(k):
-                scores(1, T, pl.multiple_of(k * TK, TK), i * TK, TQ)
-
-        if i == 0:
-            for which, index in ((0, KV_Z2B), (1, KV_Y2)):
-                arrived(piece(2, r ^ 2, which), index, when=has_two)
-                send(piece(2, r ^ 2, which), piece(2, r ^ 2, which), sibling, KV_CB2 + which, when=has_two)
-            forward_wx(1)
-            forward_wy_outer()
-
-    arrived(piece(2, r ^ 1), KV_CA2, when=has_two)
-    arrived(piece(2, r ^ 3, 0), KV_CB2, when=has_two)
-    arrived(piece(2, r ^ 3, 1), KV_CB2 + 1, when=has_two)
+    whole(1, 1, has_one)
+
+    @pl.when(has_one)
+    def _():
+        turn(1, 1)
+        before(1, 0)
+
+    for h in range(2):
+        arrived(piece(2, r ^ 2, h), KV_FAR + h, when=has_two)
+        pair_to_sibling(2, h, has_two)
+    forward_wx(1)
+    forward_wy_outer()
+
+    @pl.when(has_one)
+    def _():
+        before(1, 1)
+
+    for h in range(2):
+        whole(2, h, has_two)
 
     @pl.when(has_two)
     def _():
-        kn[2] = kv[2, 0].T
+        turn(2, 0)
+        turn(2, 1)
 
     att_x, att_y = att.at[0], att.at[1]
     x_slot, y_slot = w_rows(x, c), w_rows(y, c)
@@ -349,9 +365,10 @@
             )
         send(obuf.at[i, sub_rows(y), :], att_y.at[sub_rows(i), y_slot], sibling, A_YOWN + i)
         keep(obuf.at[i, sub_rows(y), :], att_y.at[sub_rows(i), y_slot], L_ATT + 1 + i)
-        if i == 1:
+        if i == 0:
             forward_wy_inner()
         if i == 2:
+            forward_wy_far()
             forward_x(2)
             for away in (2, 1, 3):
                 forward_y(away, 0)
@@ -359,7 +376,6 @@
         forward_x(away)
     for away in (2, 1, 3):
         forward_y(away, 1)
-    forward_wy_far()
     arrived(wx.at[w_rows(x, 1 - c), :], W_SIB)
     arrived(wy.at[w_rows(y, 1 - c), :], W_SIB + 1)
     for one in kept:
@@ -373,7 +389,9 @@
         return at(z, x, yy(step), c) if path == 0 else at(z, xx(step), y, c)
 
     def chunk_of(path, k):
-        return k * CW if path == 0 else (mine if k == 0 else theirs)
+        if path == 0:
+            return k * CW
+        return (mine if k < NC // 2 else theirs) + k % (NC // 2) * CW
 
     def sub(j, block, half):
         return part[j, sub_rows(block), half]
@@ -383,10 +401,11 @@
 
     def project(path, k):
         j = 2 * k + path
-        if path == 0:
-            arrived(wx.at[w_pair(xx(2)), pl.ds(k * CW, CW // 2)], W_FUP + k)
-            arrived(wx.at[w_pair(xx(2)), pl.ds(k * CW + CW // 2, CW // 2)], W_FDOWN + k)
-        elif k == 1:
+        if path == 0 and k * CW % WC == 0:
+            part_x = k * CW // WC
+            arrived(wx.at[w_pair(xx(2)), pl.ds(k * CW, WC // 2)], W_FUP + part_x)
+            arrived(wx.at[w_pair(xx(2)), pl.ds(k * CW + WC // 2, WC // 2)], W_FDOWN + part_x)
+        elif path == 1 and k == NC // 2:
             for group, place in enumerate((outer, inner, yy(2))):
                 arrived(wy.at[w_pair(place), col(theirs + quad, quad)], V_ZUP + group)
                 arrived(wy.at[w_pair(place), col(theirs, quad)], V_ZDOWN + group)
@@ -404,14 +423,14 @@
         send(rel.at[j, 0], rin.at[j, 0], device(path, 1), step)
         rel[j, 1] = sub(j, block_of(path, 2), right).astype(jnp.bfloat16)
         send(rel.at[j, 1], rin.at[j, 1], device(path, 3), step + 1)
+
+    def relay(path, k):
+        j = 2 * k + path
+        step = R_UP + 7 * j
         msg[j, 0] = sub(j, block_of(path, 1), right).astype(jnp.bfloat16)
         send(msg.at[j, 0], min_.at[j, 0], device(path, 1), step + 2)
         msg[j, 1] = sub(j, block_of(path, 3), left).astype(jnp.bfloat16)
         send(msg.at[j, 1], min_.at[j, 1], device(path, 3), step + 3)
-
-    def relay(path, k):
-        j = 2 * k + path
-        step = R_UP + 7 * j
         arrived(rin.at[j, 0], step)
         msg[j, 2] = (sub(j, block_of(path, 1), left) + rin[j, 0].astype(jnp.float32)).astype(jnp.bfloat16)
         send(msg.at[j, 2], min_.at[j, 2], device(path, 1), step + 4)
@@ -435,13 +454,14 @@
         send(res.at[j, other, :], place, sibling, step + 6)
 
     order = [(path, k) for k in range(NC) for path in range(2)]
-    for n in range(len(order) + 4):
-        if n < len(order):
+    lag, last = 3, len(order)
+    for n in range(2 * last):
+        if n < last:
             project(*order[n])
-        if 2 <= n < len(order) + 2:
-            relay(*order[n - 2])
-        if n >= 4:
-            finish(*order[n - 4])
+        if lag <= n < last + lag:
+            relay(*order[n - lag])
+        if n >= last:
+            finish(*order[n - last])
     for path, k in order:
         place = out_ref.at[:, col((1 - c) * HALF + path * PATH + chunk_of(path, k), CW)]
         arrived(place, R_UP + 7 * (2 * k + path) + 6)

time: 62.4 us -> 65.3 us (1.046)
  Pallas kernels: 60.3 us -> 63.3 us
    pallas_call x1, Pallas kernels: 60.3 us -> 63.3 us  [on_device(): pl.pallas_call(kernel, out_shape=jax.ShapeDtypeStruct((SUB // 2, D), bf16...]
where the time goes in v4:
time: 65.3 us; the launch traced here: 65.2 us
  Pallas kernels  63.3 us (97%)
  local copies, waits for them, and re-layouts  1.87 us (3%)
    pallas_call x1, Pallas kernels, on_device(): pl.pallas_call(kernel, out_shape=jax.ShapeDtypeStruct((SUB // 2, D), bf16...  63.3 us
    unnamed x1, local copies, waits for them, and re-layouts  1.87 us

profile of v4, /device:TPU:97, one launch (start us, length us, event | category | flops | bytes accessed | tf_op | source)
XLA Modules:
  0.0 65.2 jit_solution(3998614163282345839)
XLA Ops:
  0.0 63.3 %shard_map.55 = bf16[64,4096]{1,0:T(8,128)(2,1)} custom-call(s32[16]{0:T(128)} %starts_ref.1, bf16[2048,128]{1,0:T(8,128)(2,1)} %q_ref.1, bf16[32,2048]{1,0:T(8,128)(2,1)} %bitcast.2, bf16[32,2048]{1,0:T(8,128)(2,1)} %bitcast.3, bf16[128,4096]{1,0:T(8,128)(2,1)} %w_ref.1), custom_call_target="tpu_custom_call" | custom-call | tf_op jit(solution)/shard_map/pallas_call | solution.py:477
  63.3 1.9 %copy.7 = bf16[64,4096]{1,0:T(8,128)(2,1)} copy(bf16[64,4096]{1,0:T(8,128)(2,1)} %shard_map.55) | data formatting | bytes 1048576

commit v5 on v3

--- a/solution.py
+++ b/solution.py
@@ -173,9 +173,7 @@
         send(second, second, z_next, V_ZUP + group, when=has_next)
         send(first, first, z_prev, V_ZDOWN + group, when=has_one)
         send(second, second, z_prev, V_ZEDGE + group, V_ZUP + group, when=z == 1)
-        up = copy(first, first, z_next, V_ZEDGE + group, V_ZDOWN + group)
-        do(up.start, z == Z - 2)
-        sent.append((up, z == Z - 2))
+        send(first, first, z_next, V_ZEDGE + group, V_ZDOWN + group, when=z == Z - 2)
 
     def forward_wy_outer():
         for core in range(2):
@@ -322,15 +320,11 @@
         quarter = xx(step)
         q0 = pl.multiple_of(quarter * QT, QT)
 
-        @pl.when(has_two & (lax.rem(quarter, 2) == 1))
-        def _():
-            scores(2, 0, q0, q0, QT // 2, span=QT)
-
-        @pl.when(has_two)
-        def _():
-            @pl.loop((quarter + 1) // 2, T // TK)
-            def _(k):
-                scores(2, 0, pl.multiple_of(k * TK, TK), q0, QT // 2)
+        for place in range(X):
+
+            @pl.when(has_two & (quarter == place))
+            def _():
+                scores(2, 0, place * QT, place * QT, QT // 2, span=T - place * QT)
 
         columns = pl.ds(q0, QT)
         total = acc[HD : HD + 1, columns]
@@ -457,7 +451,7 @@
     return pl.pallas_call(
         kernel,
         out_shape=jax.ShapeDtypeStruct((SUB // 2, D), bf16),
-        in_specs=[pl.BlockSpec(memory_space=pltpu.SMEM), vmem, vmem, vmem, vmem],
+        in_specs=[pl.BlockSpec(memory_space=pltpu.SMEM), vmem, vmem, vmem, pl.BlockSpec(memory_space=pl.ANY)],
         out_specs=pl.BlockSpec(memory_space=pl.ANY),
         scratch_shapes=[
             pltpu.VMEM((3, 2, HD, T), bf16),

time: 62.4 us -> 61.3 us (0.982)
  Pallas kernels: 60.3 us -> 59.3 us
    pallas_call x1, Pallas kernels: 60.3 us -> 59.3 us  [on_device(): pl.pallas_call(kernel, out_shape=jax.ShapeDtypeStruct((SUB // 2, D), bf16...]
where the time goes in v5:
time: 61.3 us; the launch traced here: 61.2 us
  Pallas kernels  59.3 us (97%)
  local copies, waits for them, and re-layouts  1.87 us (3%)
    pallas_call x1, Pallas kernels, on_device(): pl.pallas_call(kernel, out_shape=jax.ShapeDtypeStruct((SUB // 2, D), bf16...  59.3 us
    unnamed x1, local copies, waits for them, and re-layouts  1.87 us

profile of v5, /device:TPU:97, one launch (start us, length us, event | category | flops | bytes accessed | tf_op | source)
XLA Modules:
  0.0 61.2 jit_solution(2745023273542752226)
XLA Ops:
  0.0 59.3 %shard_map.55 = bf16[64,4096]{1,0:T(8,128)(2,1)} custom-call(s32[16]{0:T(128)} %starts_ref.1, bf16[2048,128]{1,0:T(8,128)(2,1)} %q_ref.1, bf16[32,2048]{1,0:T(8,128)(2,1)} %bitcast.2, bf16[32,2048]{1,0:T(8,128)(2,1)} %bitcast.3, bf16[128,4096]{1,0:T(8,128)(2,1)} %w_ref.1), custom_call_target="tpu_custom_call" | custom-call | tf_op jit(solution)/shard_map/pallas_call | solution.py:451
  59.3 1.9 %copy.7 = bf16[64,4096]{1,0:T(8,128)(2,1)} copy(bf16[64,4096]{1,0:T(8,128)(2,1)} %shard_map.55) | data formatting | bytes 1048576

commit v6 on v5

--- a/solution.py
+++ b/solution.py
@@ -349,11 +349,11 @@
             forward_x(2)
             for away in (2, 1, 3):
                 forward_y(away, 0)
+    forward_wy_far()
     for away in (1, 3):
         forward_x(away)
     for away in (2, 1, 3):
         forward_y(away, 1)
-    forward_wy_far()
     arrived(wx.at[w_rows(x, 1 - c), :], W_SIB)
     arrived(wy.at[w_rows(y, 1 - c), :], W_SIB + 1)
     for one in kept:

time: 61.3 us -> 61 us (level)
  no operation moved by 1% of the time
where the time goes in v6:
time: 61 us; the launch traced here: 60.9 us
  Pallas kernels  59 us (97%)
  local copies, waits for them, and re-layouts  1.87 us (3%)
    pallas_call x1, Pallas kernels, on_device(): pl.pallas_call(kernel, out_shape=jax.ShapeDtypeStruct((SUB // 2, D), bf16...  59 us
    unnamed x1, local copies, waits for them, and re-layouts  1.87 us

profile of v6, /device:TPU:97, one launch (start us, length us, event | category | flops | bytes accessed | tf_op | source)
XLA Modules:
  0.0 60.9 jit_solution(1556089332077743944)
XLA Ops:
  0.0 59.0 %shard_map.55 = bf16[64,4096]{1,0:T(8,128)(2,1)} custom-call(s32[16]{0:T(128)} %starts_ref.1, bf16[2048,128]{1,0:T(8,128)(2,1)} %q_ref.1, bf16[32,2048]{1,0:T(8,128)(2,1)} %bitcast.2, bf16[32,2048]{1,0:T(8,128)(2,1)} %bitcast.3, bf16[128,4096]{1,0:T(8,128)(2,1)} %w_ref.1), custom_call_target="tpu_custom_call" | custom-call | tf_op jit(solution)/shard_map/pallas_call | solution.py:451
  59.0 1.9 %copy.7 = bf16[64,4096]{1,0:T(8,128)(2,1)} copy(bf16[64,4096]{1,0:T(8,128)(2,1)} %shard_map.55) | data formatting | bytes 1048576
